TPU v7x, 128 devices: a whole 4x4x4 slice. The times are simulated.
128 devices in a mesh: seq: 8 (over z, core), head: 16 (over x, y).
Axes of the slice: x: 4, y: 4, z: 4, core: 2. Of those that a mesh axis runs over, the one named last changes fastest.
Arguments:
- hidden_in: float32 [2048, 1536], P('seq'), may hold values from -6 to 6
- norm_gain: float32 [2, 1536], replicated, may hold values from 0.1 to 1.9
- gate_mixer_weight: bfloat16 [2, 1536, 2, 3072], P(None, None, None, 'head'), may hold values from -0.15625 to 0.15625
- w_bc: bfloat16 [2, 1536, 256], replicated, may hold values from -0.15625 to 0.15625
- w_dt: bfloat16 [2, 1536, 48], P(None, None, 'head'), may hold values from -0.15625 to 0.15625
- conv_x: float32 [2, 5, 3072], P(None, None, 'head'), may hold values from -3 to 3
- conv_bc: float32 [2, 5, 256], replicated, may hold values from -3 to 3
- head_params: float32 [2, 3, 48], P(None, None, 'head'), as said below
- gate_gain: float32 [2, 3072], P(None, 'head'), may hold values from 0.1 to 1.9
- w_out: bfloat16 [2, 3072, 1536], P(None, 'head'), may hold values from -0.109375 to 0.109375
- out_grad: float32 [2048, 1536], P('seq'), may hold values from -6 to 6
Outputs:
- hidden_out: float32 [2048, 1536], P('seq', 'head')
- grad_in: float32 [2048, 1536], P('seq', 'head')
- grad_norm_gain: float32 [2, 1536], P(None, 'head')
- grad_w_zx: float32 [2, 1536, 2, 3072], P(None, 'seq', None, 'head')
- grad_w_bc: float32 [2, 1536, 256], P(None, 'seq')
- grad_w_dt: float32 [2, 1536, 48], P(None, 'seq', 'head')
- grad_conv_x: float32 [2, 5, 3072], P(None, None, 'head')
- grad_conv_bc: float32 [2, 5, 256], replicated
- grad_head_params: float32 [2, 3, 48], P(None, None, 'head')
- grad_gate_gain: float32 [2, 3072], P(None, 'head')
- grad_w_out: float32 [2, 3072, 1536], P(None, 'head', 'seq')
Inputs may be any that keep to these rules, and one draw needn't show every extreme that they name: `head_params`: rows per layer: each head's time-step bias, log decay rate and skip weight.
All inputs are finite; a program needn't handle non-finite values.
Results may differ from a plain program's by a relative error of at most 0.017.
Values may be sent and summed in bfloat16 or wider, within the bound.
A program may use at most 128 MiB of HBM per device.

v0:
```python
import math

import jax
import jax.numpy as jnp
from jax import lax
from jax.sharding import Mesh
from jax.sharding import PartitionSpec as P

INNER = 3072
HEAD = ("head_0", "head_1")


EPSILON = 1e-05
TOP_PRECISION = lax.Precision.HIGHEST


def passed_along(value, axis, steps):
    count = lax.axis_size(axis)
    initial, last = (max(0, -steps), min(count, count - steps))
    return lax.ppermute(value, axis, [(source, source + steps) for source in range(initial, last)])


def from_everyone(x, axis):
    length = lax.axis_size(axis)
    return lax.all_to_all(jnp.broadcast_to(x[None], (length, *x.shape)), axis, 0, 0, tiled=True)


def combined_pairwise(pieces, combine):
    while len(jax.tree.leaves(pieces)[0]) > 1:
        pieces = jax.vmap(combine)(
            *(jax.tree.map(lambda part: part[side::2], pieces) for side in (0, 1))
        )
    return jax.tree.map(lambda part: part[0], pieces)


def carried_in(x, axis, combine, identity, reverse):
    length, position = (lax.axis_size(axis), lax.axis_index(axis))
    passed = jnp.arange(length) > position if reverse else jnp.arange(length) < position

    def kept(part, zero, own):
        part = jnp.where(
            passed.reshape(-1, *(1 for _ in own.shape)), part, jnp.asarray(zero, own.dtype)
        )
        return part[::-1] if reverse else part

    pieces = jax.tree.map(lambda part: from_everyone(part, axis), x)
    return combined_pairwise(jax.tree.map(kept, pieces, identity, x), combine)


def over_axes(x, axes):
    for axis in axes:
        x = lax.psum(x, axis)
    return x


def over_copies(x, axis):
    return from_everyone(x, axis).sum(axis=0)


def packed_total(arrays, axis):
    ends = [0]
    for a in arrays:
        ends.append(ends[-1] + a.size)
    running = over_copies(jnp.concatenate([a.ravel() for a in arrays]), axis)
    return tuple((running[b:e].reshape(a.shape) for a, b, e in zip(arrays, ends, ends[1:])))


def in_one_piece(arrays, axis, dim, along):
    columns = [a.reshape(*a.shape[:along], -1) for a in arrays]
    both = jnp.concatenate(columns, axis=along)
    whole, at, finished = (lax.all_gather(both, axis, axis=dim, tiled=True), 0, [])
    for a, column in zip(arrays, columns):
        piece = whole[..., at : at + column.shape[along]]
        finished.append(piece.reshape(*piece.shape[:along], *a.shape[along:]))
        at += column.shape[along]
    return tuple(finished)


def norm_rows(residual, gain_row):
    return (
        residual
        * lax.rsqrt(jnp.mean(residual * residual, axis=1, keepdims=True) + EPSILON)
        * gain_row
    )


def conv_act(joined, prev_rim, conv_weight, step_raw, head_rows):
    length = joined.shape[0]
    tap_count = conv_weight.shape[0] - 1
    extended = jnp.concatenate([prev_rim, joined], axis=0)
    preact = conv_weight[tap_count]
    for index_tap in range(tap_count):
        preact = preact + conv_weight[index_tap] * extended[index_tap : index_tap + length]
    time_step = jax.nn.softplus(step_raw + head_rows[0])
    return (jax.nn.silu(preact), time_step, -time_step * jnp.exp(head_rows[1]))


def block_scan(carry_state, pieces):
    inputs, time_step, decay_log, b_matrix, c_matrix = pieces
    block_size = decay_log.shape[0]
    cumulative = jnp.cumsum(decay_log, axis=0)
    cum_heads = jnp.transpose(cumulative)
    causal = (
        lax.broadcasted_iota(jnp.int32, (block_size, block_size), 0)
        >= lax.broadcasted_iota(jnp.int32, (block_size, block_size), 1)
    )[None, :, :]
    segment = jnp.where(
        causal, jnp.exp(jnp.where(causal, cum_heads[:, :, None] - cum_heads[:, None, :], 0.0)), 0.0
    )
    scores = jnp.einsum(
        "tn,sn->ts",
        c_matrix.astype(jnp.bfloat16),
        b_matrix.astype(jnp.bfloat16),
        preferred_element_type=jnp.float32,
    )
    weights = scores[None, :, :] * segment * jnp.transpose(time_step)[:, None, :]
    inner = jnp.einsum(
        "hts,hsp->htp", weights, jnp.transpose(inputs, (1, 0, 2)), precision=TOP_PRECISION
    )
    output = jnp.transpose(inner, (1, 0, 2)) + jnp.exp(cumulative)[:, :, None] * jnp.einsum(
        "tn,hpn->thp", c_matrix, carry_state, precision=TOP_PRECISION
    )
    tail_weight = jnp.exp(cumulative[-1][None, :] - cumulative) * time_step
    next_state = jnp.exp(cumulative[-1])[:, None, None] * carry_state + jnp.einsum(
        "sh,shp,sn->hpn", tail_weight, inputs, b_matrix, precision=TOP_PRECISION
    )
    return (next_state, output)


def ssd_zero(inputs, time_step, decay_log, b_matrix, c_matrix):
    length, head_count, head_dim = inputs.shape
    block_size = math.gcd(length, 256)
    block_count = length // block_size
    pieces = (
        inputs.reshape(block_count, block_size, head_count, head_dim),
        time_step.reshape(block_count, block_size, head_count),
        decay_log.reshape(block_count, block_size, head_count),
        b_matrix.reshape(block_count, block_size, -1),
        c_matrix.reshape(block_count, block_size, -1),
    )
    begin_state = jnp.zeros((head_count, head_dim, b_matrix.shape[1]), jnp.float32)
    final_state, outputs = lax.scan(block_scan, begin_state, pieces)
    return (
        outputs.reshape(length, head_count, head_dim),
        final_state,
        jnp.cumsum(decay_log, axis=0),
    )


def gate_in(y_zero, cumulative, state_in, c_matrix, inputs, head_rows, z_part):
    length = inputs.shape[0]
    carried = jnp.exp(cumulative)[:, :, None] * jnp.einsum(
        "tn,hpn->thp", c_matrix, state_in, precision=TOP_PRECISION
    )
    y_full = y_zero + carried + head_rows[2][None, :, None] * inputs
    gated_rows = y_full.reshape(length, -1) * jax.nn.silu(z_part)
    return (gated_rows, jnp.sum(gated_rows * gated_rows, axis=1))


def gate_out(gated_rows, total_squares, gain_row):
    return gated_rows * lax.rsqrt(total_squares / INNER + EPSILON)[:, None] * gain_row


def chain_step(earlier, later_part):
    return (later_part[0] * earlier[0], later_part[0][:, None, None] * earlier[1] + later_part[1])


def on_device(
    hidden_in,
    norm_gain,
    gate_mixer_weight,
    w_bc,
    w_dt,
    conv_x,
    conv_bc,
    head_params,
    gate_gain,
    w_out,
    out_grad,
):
    length = hidden_in.shape[0]
    model_width = hidden_in.shape[1]
    local_inner = gate_gain.shape[1]
    local_heads = head_params.shape[2]
    head_dim = local_inner // local_heads
    state_dim = w_bc.shape[2] // 2
    layer_count = gate_mixer_weight.shape[0]
    rim_rows = conv_x.shape[1] - 2
    share_width = model_width // lax.axis_size(HEAD)
    share_start = lax.axis_index(HEAD) * share_width
    residual = hidden_in
    kept_items = []
    for index_of_layer in range(layer_count):
        normalized_rows, back_norm = jax.vjp(norm_rows, residual, norm_gain[index_of_layer])
        normalized_lower = normalized_rows.astype(jnp.bfloat16)
        projection_output = jnp.einsum(
            "np,pwg->nwg",
            normalized_lower,
            gate_mixer_weight[index_of_layer],
            preferred_element_type=jnp.float32,
        )
        bc_raw = jnp.dot(normalized_lower, w_bc[index_of_layer], preferred_element_type=jnp.float32)
        step_raw = jnp.dot(
            normalized_lower, w_dt[index_of_layer], preferred_element_type=jnp.float32
        )
        joined = jnp.concatenate([projection_output[:, 1], bc_raw], axis=1)
        prev_rim = passed_along(joined[length - rim_rows :], "seq", 1)
        conv_weight = jnp.concatenate([conv_x[index_of_layer], conv_bc[index_of_layer]], axis=1)
        (activated, time_step, decay_log), back_conv = jax.vjp(
            conv_act, joined, prev_rim, conv_weight, step_raw, head_params[index_of_layer]
        )
        inputs = activated[:, :local_inner].reshape(length, local_heads, head_dim)
        b_matrix = (
            activated[:, local_inner : local_inner + state_dim]
            .astype(jnp.bfloat16)
            .astype(jnp.float32)
        )
        c_matrix = activated[:, local_inner + state_dim :].astype(jnp.bfloat16).astype(jnp.float32)
        (y_zero, local_state, cumulative), back_ssd = jax.vjp(
            ssd_zero, inputs, time_step, decay_log, b_matrix, c_matrix
        )
        decay_total = jnp.exp(cumulative[-1])
        identity = (jnp.ones_like(decay_total), jnp.zeros_like(local_state))
        state_in = carried_in((decay_total, local_state), "seq", chain_step, identity, False)[1]
        (gated_rows, squares), back_gate_in = jax.vjp(
            gate_in,
            y_zero,
            cumulative,
            state_in,
            c_matrix,
            inputs,
            head_params[index_of_layer],
            projection_output[:, 0],
        )
        total_squares = over_axes(squares, HEAD)
        gate_normed, back_gate_out = jax.vjp(
            gate_out, gated_rows, total_squares, gate_gain[index_of_layer]
        )
        gate_low = gate_normed.astype(jnp.bfloat16)
        mixer_term = jnp.dot(gate_low, w_out[index_of_layer], preferred_element_type=jnp.float32)
        residual = residual + lax.psum(mixer_term, HEAD)
        kept_items.append(
            (
                back_norm,
                normalized_lower,
                back_conv,
                back_ssd,
                decay_total,
                state_in,
                back_gate_in,
                back_gate_out,
                gate_low,
            )
        )
    grad_resid = out_grad
    small_grads = [None] * layer_count
    large_grads = [None] * layer_count
    for index_of_layer in range(layer_count - 1, -1, -1):
        (
            back_norm,
            normalized_lower,
            back_conv,
            back_ssd,
            decay_total,
            state_in,
            back_gate_in,
            back_gate_out,
            gate_low,
        ) = kept_items[index_of_layer]
        grad_mix = grad_resid.astype(jnp.bfloat16)
        grad_gate = jnp.einsum(
            "td,id->ti", grad_mix, w_out[index_of_layer], preferred_element_type=jnp.float32
        )
        grad_gated, grad_squares, grad_ggain = back_gate_out(grad_gate)
        grad_squares = over_axes(grad_squares, HEAD)
        (
            grad_yzero,
            grad_cumulative,
            grad_state_in,
            grad_cfirst,
            grad_infirst,
            grad_rows_gate,
            grad_z,
        ) = back_gate_in((grad_gated, grad_squares))
        identity = (jnp.ones_like(decay_total), jnp.zeros_like(grad_state_in))
        state_grad_next = carried_in(
            (decay_total, grad_state_in), "seq", chain_step, identity, True
        )[1]
        grad_total = decay_total * jnp.sum(state_grad_next * state_in, axis=(1, 2))
        grad_cumulative = grad_cumulative.at[-1].add(grad_total)
        grad_insecond, grad_step, grad_decay_log, grad_b, grad_csecond = back_ssd(
            (grad_yzero, state_grad_next, grad_cumulative)
        )
        grad_act = jnp.concatenate(
            [
                (grad_infirst + grad_insecond).reshape(length, local_inner),
                grad_b,
                grad_cfirst + grad_csecond,
            ],
            axis=1,
        )
        grad_joined, grad_rim, grad_conv, grad_step_raw, grad_rows_conv = back_conv(
            (grad_act, grad_step, grad_decay_log)
        )
        grad_next_rim = passed_along(grad_rim, "seq", -1)
        grad_joined = grad_joined.at[length - rim_rows :].add(grad_next_rim)
        grad_bc, grad_conv_bc = packed_total(
            (grad_joined[:, local_inner:], grad_conv[:, local_inner:]), HEAD
        )
        projection_gradient_lower = jnp.stack(
            [grad_z, grad_joined[:, :local_inner]], axis=1
        ).astype(jnp.bfloat16)
        grad_bc_low = grad_bc.astype(jnp.bfloat16)
        grad_step_low = grad_step_raw.astype(jnp.bfloat16)
        grad_normed = jnp.einsum(
            "vzy,jzy->vj",
            projection_gradient_lower,
            gate_mixer_weight[index_of_layer],
            preferred_element_type=jnp.float32,
        )
        grad_normed = grad_normed + jnp.einsum(
            "th,dh->td", grad_step_low, w_dt[index_of_layer], preferred_element_type=jnp.float32
        )
        grad_normed = lax.psum(grad_normed, HEAD) + jnp.einsum(
            "tn,dn->td", grad_bc_low, w_bc[index_of_layer], preferred_element_type=jnp.float32
        )
        grad_back_resid, grad_full_gain = back_norm(grad_normed)
        grad_resid = grad_resid + grad_back_resid
        grad_ngain = lax.dynamic_slice_in_dim(grad_full_gain, share_start, share_width, 0)
        small_grads[index_of_layer] = (
            grad_ngain,
            grad_conv[:, :local_inner],
            grad_conv_bc,
            grad_rows_gate + grad_rows_conv,
            grad_ggain,
        )
        normed_rows, mix_rows = (
            lax.all_to_all(normalized_lower, "seq", split_axis=1, concat_axis=0, tiled=True),
            lax.all_to_all(grad_mix, "seq", split_axis=1, concat_axis=0, tiled=True),
        )
        pieces = in_one_piece(
            (projection_gradient_lower, grad_step_low, grad_bc_low, gate_low), "seq", 0, 1
        )
        large_grads[index_of_layer] = (
            jnp.einsum("ap,ajz->pjz", normed_rows, pieces[0], preferred_element_type=jnp.float32),
            jnp.einsum("td,tn->dn", normed_rows, pieces[2], preferred_element_type=jnp.float32),
            jnp.einsum("td,th->dh", normed_rows, pieces[1], preferred_element_type=jnp.float32),
            jnp.einsum("ti,td->id", pieces[3], mix_rows, preferred_element_type=jnp.float32),
        )
    stacked_small = tuple(
        (jnp.stack([entry_list[position] for entry_list in small_grads]) for position in range(5))
    )
    stacked_large = tuple(
        (jnp.stack([entry_list[position] for entry_list in large_grads]) for position in range(4))
    )
    grad_ngain, grad_convx, grad_convbc, grad_heads, grad_ggain = packed_total(
        (stacked_small[0], stacked_small[1], stacked_small[2], stacked_small[3], stacked_small[4]),
        "seq",
    )
    grad_wzx, grad_wbc, grad_wdt, grad_wout = stacked_large
    out_share = lax.dynamic_slice_in_dim(residual, share_start, share_width, 1)
    grad_share = lax.dynamic_slice_in_dim(grad_resid, share_start, share_width, 1)
    return (
        out_share,
        grad_share,
        grad_ngain,
        grad_wzx,
        grad_wbc,
        grad_wdt,
        grad_convx,
        grad_convbc,
        grad_heads,
        grad_ggain,
        grad_wout,
    )


def solution(mesh):
    split = Mesh(mesh.devices.reshape(mesh.shape["seq"], 4, 4), ("seq", "head_0", "head_1"))
    placed = (
        P("seq", None),
        P(),
        P(None, None, None, HEAD),
        P(),
        P(None, None, HEAD),
        P(None, None, HEAD),
        P(),
        P(None, None, HEAD),
        P(None, HEAD),
        P(None, HEAD, None),
        P("seq", None),
    )
    return jax.shard_map(
        on_device,
        mesh=split,
        in_specs=placed,
        out_specs=(
            P("seq", HEAD),
            P("seq", HEAD),
            P(None, HEAD),
            P(None, "seq", None, HEAD),
            P(None, "seq", None),
            P(None, "seq", HEAD),
            P(None, None, HEAD),
            P(),
            P(None, None, HEAD),
            P(None, HEAD),
            P(None, HEAD, "seq"),
        ),
        check_vma=False,
    )
```

profile of v0, /device:TPU:1, one launch (start us, length us, event | category | flops | bytes accessed | tf_op | source)
XLA Modules:
  0.0 773.1 jit_solution(16147404223580523794)
XLA Ops:
  44.9 9.1 %all-to-all-done.1 = f32[8,3,64,128]{3,2,1,0:T(8,128)S(1)} async-done(((f32[8,3,64,128]{3,2,1,0:T(8,128)}), f32[8,3,64,128]{3,2,1,0:T(8,128)S(1)}, u32[]{:S(2)}, u32[]{:S(2)}) %all-to-all-start.1) | async-done | bytes 786464 | tf_op jit(solution)/shard_map/all_to_all | solution.py:25
  58.3 8.4 %psum.84 = f32[256]{0:T(256)S(1)} all-reduce(f32[256]{0:T(256)S(1)} %get-tuple-element.940), channel_id=1, replica_groups=mesh['seq'=8,'head_0'=4,'head_1'=4] {'head_0'}, use_global_device_ids=true, to_apply=%region_4.6 | all-reduce | flops 256 | bytes 2048 | tf_op jit(solution)/shard_map/psum | solution.py:52
  66.7 8.7 %psum.85 = f32[256]{0:T(256)S(1)} all-reduce(f32[256]{0:T(256)S(1)} %psum.84), channel_id=1, replica_groups=mesh['seq'=8,'head_0'=4,'head_1'=4] {'head_1'}, use_global_device_ids=true, to_apply=%region_5.7 | all-reduce | flops 256 | bytes 2048 | tf_op jit(solution)/shard_map/psum | solution.py:52
  80.9 83.8 %all-reduce.33.cloned.1.call-done = f32[256,1536]{1,0:T(8,128)} async-done(((f32[256,1536]{1,0:T(8,128)}), f32[256,1536]{1,0:T(8,128)}) %all-reduce.33.cloned.1.call-update) | async-done | bytes 1572880 | tf_op jit(solution)/shard_map/psum | solution.py:241
  173.8 6.5 all-to-all-start.2
  196.9 5.7 all-to-all-start.3
  207.0 7.9 %all-to-all-done.3 = f32[8,3,64,128]{3,2,1,0:T(8,128)} async-done(((f32[8,3,64,128]{3,2,1,0:T(8,128)}), f32[8,3,64,128]{3,2,1,0:T(8,128)}, u32[]{:S(2)}, u32[]{:S(2)}) %all-to-all-start.3) | async-done | bytes 786464 | tf_op jit(solution)/shard_map/all_to_all | solution.py:25
  220.3 8.1 %psum.87 = f32[256]{0:T(256)S(1)} all-reduce(f32[256]{0:T(256)S(1)} %get-tuple-element.933), channel_id=1, replica_groups=mesh['seq'=8,'head_0'=4,'head_1'=4] {'head_0'}, use_global_device_ids=true, to_apply=%region_11.13 | all-reduce | flops 256 | bytes 2048 | tf_op jit(solution)/shard_map/psum | solution.py:52
  228.4 6.9 psum.88
  240.6 6.8 psum.90
  247.4 6.0 psum.91
  258.1 12.7 %all-to-all-start.4 = ((f32[8,3,64,128]{3,2,1,0:T(8,128)}), f32[8,3,64,128]{3,2,1,0:T(8,128)}, u32[]{:S(2)}, u32[]{:S(2)}) async-start(f32[8,3,64,128]{3,2,1,0:T(8,128)} %broadcast_in_dim.476), calls=%async_computation.4 | async-start | bytes 1572864 | tf_op jit(solution)/shard_map/all_to_all | solution.py:25
  275.1 8.2 %all-to-all-done.4 = f32[8,3,64,128]{3,2,1,0:T(8,128)} async-done(((f32[8,3,64,128]{3,2,1,0:T(8,128)}), f32[8,3,64,128]{3,2,1,0:T(8,128)}, u32[]{:S(2)}, u32[]{:S(2)}) %all-to-all-start.4) | async-done | bytes 786464 | tf_op jit(solution)/shard_map/all_to_all | solution.py:25
  353.1 20.0 %all-to-all-done.5 = f32[16,1,66816]{2,1,0:T(1,128)} async-done(((f32[16,1,66816]{2,1,0:T(1,128)}), f32[16,1,66816]{2,1,0:T(1,128)}, u32[]{:S(2)}, u32[]{:S(2)}) %all-to-all-start.5) | async-done | bytes 4276256 | tf_op jit(solution)/shard_map/all_to_all | solution.py:25
  381.2 71.2 %all-reduce.35.cloned.1.call-done = f32[256,1536]{1,0:T(8,128)} async-done(((f32[256,1536]{1,0:T(8,128)}), f32[256,1536]{1,0:T(8,128)}) %all-reduce.35.cloned.1.call-update) | async-done | bytes 1572880 | tf_op jit(solution)/shard_map/psum | solution.py:324
  460.2 7.9 %psum.93 = f32[256]{0:T(256)} all-reduce(f32[256]{0:T(256)} %multiply_multiply_fusion.5), channel_id=1, replica_groups=mesh['seq'=8,'head_0'=4,'head_1'=4] {'head_0'}, use_global_device_ids=true, to_apply=%region_39.41 | all-reduce | flops 256 | bytes 2048 | tf_op jit(solution)/shard_map/psum | solution.py:52
  468.1 8.1 %psum.94 = f32[256]{0:T(256)} all-reduce(f32[256]{0:T(256)} %psum.93), channel_id=1, replica_groups=mesh['seq'=8,'head_0'=4,'head_1'=4] {'head_1'}, use_global_device_ids=true, to_apply=%region_40.42 | all-reduce | flops 256 | bytes 2048 | tf_op jit(solution)/shard_map/psum | solution.py:52
  484.8 10.7 %all-to-all-start.6 = ((f32[8,3,64,128]{3,2,1,0:T(8,128)}), f32[8,3,64,128]{3,2,1,0:T(8,128)}, u32[]{:S(2)}, u32[]{:S(2)}) async-start(f32[8,3,64,128]{3,2,1,0:T(8,128)} %broadcast_in_dim.480), calls=%async_computation.6 | async-start | bytes 1572864 | tf_op jit(solution)/shard_map/all_to_all | solution.py:25
  501.2 6.7 all-to-all-done.6
  558.5 71.7 %all-to-all-done.7 = f32[16,1,66816]{2,1,0:T(1,128)} async-done(((f32[16,1,66816]{2,1,0:T(1,128)}), f32[16,1,66816]{2,1,0:T(1,128)}, u32[]{:S(2)}, u32[]{:S(2)}) %all-to-all-start.7) | async-done | bytes 4276256 | tf_op jit(solution)/shard_map/all_to_all | solution.py:25
  647.4 10.1 %all-to-all-done.12 = bf16[256,8,192]{0,2,1:T(8,128)(2,1)} async-done(((bf16[256,8,192]{0,2,1:T(8,128)(2,1)}), bf16[256,8,192]{0,2,1:T(8,128)(2,1)}, u32[]{:S(2)}, u32[]{:S(2)}) %all-to-all-start.12) | async-done | bytes 786464 | tf_op jit(solution)/shard_map/all_to_all | solution.py:339
  664.9 10.0 %all-to-all-done.9 = bf16[256,8,192]{0,2,1:T(8,128)(2,1)} async-done(((bf16[256,8,192]{0,2,1:T(8,128)(2,1)}), bf16[256,8,192]{0,2,1:T(8,128)(2,1)}, u32[]{:S(2)}, u32[]{:S(2)}) %all-to-all-start.9) | async-done | bytes 786464 | tf_op jit(solution)/shard_map/all_to_all | solution.py:338
  682.2 10.1 %all-to-all-done.10 = bf16[256,8,192]{0,2,1:T(8,128)(2,1)} async-done(((bf16[256,8,192]{0,2,1:T(8,128)(2,1)}), bf16[256,8,192]{0,2,1:T(8,128)(2,1)}, u32[]{:S(2)}, u32[]{:S(2)}) %all-to-all-start.10) | async-done | bytes 786464 | tf_op jit(solution)/shard_map/all_to_all | solution.py:338
  744.6 12.7 %all-gather.3.cloned.1.call-done = bf16[2048,835]{0,1:T(8,128)(2,1)} async-done(((bf16[256,835]{0,1:T(8,128)(2,1)}), bf16[2048,835]{0,1:T(8,128)(2,1)}) %all-gather.3.cloned.1.call-update) | async-done | bytes 3420176 | tf_op jit(solution)/shard_map/all_gather | solution.py:71
  (807 shorter events, 338.2 us)
Async XLA Ops:
  15.3 17.7 %collective-permute-start = (f32[3,448]{0,1:T(8,128)}, f32[3,448]{0,1:T(8,128)}, u32[]{:S(2)}, u32[]{:S(2)}) collective-permute-start(f32[3,448]{0,1:T(8,128)} %fusion.92), channel_id=1, source_target_pairs={{0,16},{16,32},{32,48},{48,64},{64,80},{80,96},{96,112},{1,17},{17... | collective-permute-start | bytes 16136 | tf_op jit(solution)/shard_map/ppermute | solution.py:20
  20.9 146.1 %copy-start.84 = (bf16[1,1536,3]{1,0,2:T(2,128)(2,1)}, bf16[1,1536,3]{1,0,2:T(2,128)(2,1)S(1)}, u32[]{:S(2)}) copy-start(bf16[1,1536,3]{1,0,2:T(2,128)(2,1)S(1)} %get-tuple-element.967) | copy-start | bytes 27652
  23.4 9.5 %all-to-all-start = ((f32[8,1,3]{2,1,0:T(1,128)}), f32[8,1,3]{2,1,0:T(1,128)S(1)}, u32[]{:S(2)}, u32[]{:S(2)}) async-start(f32[8,1,3]{2,1,0:T(1,128)} %broadcast_in_dim.466), calls=%async_computation | async-start | bytes 8192 | tf_op jit(solution)/shard_map/all_to_all | solution.py:25
  29.1 241.8 %copy-start.89 = (pred[256,256]{1,0:T(8,128)(4,1)}, pred[256,256]{1,0:T(8,128)(4,1)S(1)}, u32[]{:S(2)}) copy-start(pred[256,256]{1,0:T(8,128)(4,1)S(1)} %iota_compare_fusion) | copy-start | bytes 196612
  37.6 16.5 %all-to-all-start.1 = ((f32[8,3,64,128]{3,2,1,0:T(8,128)}), f32[8,3,64,128]{3,2,1,0:T(8,128)S(1)}, u32[]{:S(2)}, u32[]{:S(2)}) async-start(f32[8,3,64,128]{3,2,1,0:T(8,128)} %broadcast_in_dim.469), calls=%async_computation.1 | async-start | bytes 1572864 | tf_op jit(solution)/shard_map/all_to_all | solution.py:25
  41.7 123.0 %all-reduce.33.cloned.1.call-start = ((), (), s32[]{:S(2)}) async-start(), calls=%async_computation.13 | async-start | bytes 3145728 | tf_op jit(solution)/shard_map/psum | solution.py:241
  173.8 13.7 %all-to-all-start.2 = ((f32[8,1,3]{2,1,0:T(1,128)}), f32[8,1,3]{2,1,0:T(1,128)S(1)}, u32[]{:S(2)}, u32[]{:S(2)}) async-start(f32[8,1,3]{2,1,0:T(1,128)} %broadcast_in_dim.471), calls=%async_computation.2 | async-start | bytes 8192 | tf_op jit(solution)/shard_map/all_to_all | solution.py:25
  184.0 6.8 collective-permute-start.1
  196.9 18.1 %all-to-all-start.3 = ((f32[8,3,64,128]{3,2,1,0:T(8,128)}), f32[8,3,64,128]{3,2,1,0:T(8,128)}, u32[]{:S(2)}, u32[]{:S(2)}) async-start(f32[8,3,64,128]{3,2,1,0:T(8,128)} %broadcast_in_dim.472), calls=%async_computation.3 | async-start | bytes 1572864 | tf_op jit(solution)/shard_map/all_to_all | solution.py:25
  258.1 25.1 %all-to-all-start.4 = ((f32[8,3,64,128]{3,2,1,0:T(8,128)}), f32[8,3,64,128]{3,2,1,0:T(8,128)}, u32[]{:S(2)}, u32[]{:S(2)}) async-start(f32[8,3,64,128]{3,2,1,0:T(8,128)} %broadcast_in_dim.476), calls=%async_computation.4 | async-start | bytes 1572864 | tf_op jit(solution)/shard_map/all_to_all | solution.py:25
  292.8 7.6 collective-permute-start.2
  313.1 60.0 %all-to-all-start.5 = ((f32[16,1,66816]{2,1,0:T(1,128)}), f32[16,1,66816]{2,1,0:T(1,128)}, u32[]{:S(2)}, u32[]{:S(2)}) async-start(f32[16,1,66816]{2,1,0:T(1,128)} %broadcast_in_dim.477), calls=%async_computation.5 | async-start | bytes 8552448 | tf_op jit(solution)/shard_map/all_to_all | solution.py:25
  317.6 134.7 %all-reduce.35.cloned.1.call-start = ((), (), s32[]{:S(2)}) async-start(), calls=%async_computation.14 | async-start | bytes 3145728 | tf_op jit(solution)/shard_map/psum | solution.py:324
  484.8 23.1 %all-to-all-start.6 = ((f32[8,3,64,128]{3,2,1,0:T(8,128)}), f32[8,3,64,128]{3,2,1,0:T(8,128)}, u32[]{:S(2)}, u32[]{:S(2)}) async-start(f32[8,3,64,128]{3,2,1,0:T(8,128)} %broadcast_in_dim.480), calls=%async_computation.6 | async-start | bytes 1572864 | tf_op jit(solution)/shard_map/all_to_all | solution.py:25
  495.5 223.9 %all-reduce.37.cloned.1.call-start = ((), (), s32[]{:S(2)}) async-start(), calls=%async_computation.17 | async-start | bytes 6291456 | tf_op jit(solution)/shard_map/psum | solution.py:241
  517.5 17.0 %collective-permute-start.3 = (f32[3,448]{0,1:T(8,128)S(1)}, f32[3,448]{0,1:T(8,128)}, u32[]{:S(2)}, u32[]{:S(2)}) collective-permute-start(f32[3,448]{0,1:T(8,128)S(1)} %split.19), channel_id=1, source_target_pairs={{16,0},{32,16},{48,32},{64,48},{80,64},{96,80},{112,96},{17,1},{33... | collective-permute-start | bytes 16136 | tf_op jit(solution)/shard_map/ppermute | solution.py:20
  542.7 195.5 %all-gather.5.cloned.1.call-start = ((), (), s32[]{:S(2)}) async-start(), calls=%async_computation.16 | async-start | bytes 3870720 | tf_op jit(solution)/shard_map/all_gather | solution.py:71
  553.5 76.7 %all-to-all-start.7 = ((f32[16,1,66816]{2,1,0:T(1,128)}), f32[16,1,66816]{2,1,0:T(1,128)}, u32[]{:S(2)}, u32[]{:S(2)}) async-start(f32[16,1,66816]{2,1,0:T(1,128)} %broadcast_in_dim.481), calls=%async_computation.7 | async-start | bytes 8552448 | tf_op jit(solution)/shard_map/all_to_all | solution.py:25
  558.2 199.0 %all-gather.3.cloned.1.call-start = ((), (), s32[]{:S(2)}) async-start(), calls=%async_computation.15 | async-start | bytes 3870720 | tf_op jit(solution)/shard_map/all_gather | solution.py:71
  640.9 16.7 %all-to-all-start.12 = ((bf16[256,8,192]{0,2,1:T(8,128)(2,1)}), bf16[256,8,192]{0,2,1:T(8,128)(2,1)}, u32[]{:S(2)}, u32[]{:S(2)}) async-start(bf16[256,8,192]{0,2,1:T(8,128)(2,1)} %bitcast.641), calls=%async_computation.12 | async-start | bytes 1572864 | tf_op jit(solution)/shard_map/all_to_all | solution.py:339
  657.6 17.4 %all-to-all-start.9 = ((bf16[256,8,192]{0,2,1:T(8,128)(2,1)}), bf16[256,8,192]{0,2,1:T(8,128)(2,1)}, u32[]{:S(2)}, u32[]{:S(2)}) async-start(bf16[256,8,192]{0,2,1:T(8,128)(2,1)} %bitcast.627), calls=%async_computation.9 | async-start | bytes 1572864 | tf_op jit(solution)/shard_map/all_to_all | solution.py:338
  674.9 17.4 %all-to-all-start.10 = ((bf16[256,8,192]{0,2,1:T(8,128)(2,1)}), bf16[256,8,192]{0,2,1:T(8,128)(2,1)}, u32[]{:S(2)}, u32[]{:S(2)}) async-start(bf16[256,8,192]{0,2,1:T(8,128)(2,1)} %bitcast.628), calls=%async_computation.10 | async-start | bytes 1572864 | tf_op jit(solution)/shard_map/all_to_all | solution.py:338
  692.3 23.9 %all-to-all-start.11 = ((bf16[256,8,192]{0,2,1:T(8,128)(2,1)}), bf16[256,8,192]{0,2,1:T(8,128)(2,1)}, u32[]{:S(2)}, u32[]{:S(2)}) async-start(bf16[256,8,192]{0,2,1:T(8,128)(2,1)} %bitcast.626), calls=%async_computation.11 | async-start | bytes 1572864 | tf_op jit(solution)/shard_map/all_to_all | solution.py:339
  724.6 9.9 %all-to-all-start.8 = ((f32[8,1,5074]{2,1,0:T(1,128)}), f32[8,1,5074]{2,1,0:T(1,128)S(1)}, u32[]{:S(2)}, u32[]{:S(2)}) async-start(f32[8,1,5074]{2,1,0:T(1,128)} %broadcast_in_dim.485), calls=%async_computation.8 | async-start | bytes 327680 | tf_op jit(solution)/shard_map/all_to_all | solution.py:25
  (212 other events, 1785.2 us)
Sparse Core Ops, SparseCore 0:
  78.5 86.2 all-reduce.32
  343.6 108.7 all-reduce.34
  542.7 136.9 all-reduce.36
  681.3 39.7 all-gather.4
  722.7 34.5 all-gather.2
where the time goes:
time: 786 us; the launch traced here: 773 us
  waiting for transfers between devices  333 us (42%)
  local copies, waits for them, and re-layouts  111 us (14%)
  other arithmetic  92.6 us (12%)
  starting transfers between devices  91.9 us (12%)
  matrix products  67.5 us (9%)
  blocking collectives  60.9 us (8%)
  between operations  16.9 us (2%)
    all_to_all x9, waiting for transfers between devices, from_everyone(): lax.all_to_all(jnp.broadcast_to(x[None], (length, *x.shape)), axis, 0, 0,...  128 us
    psum x2, waiting for transfers between devices, on_device(): residual = residual + lax.psum(mixer_term, HEAD)  83.8 us
    psum x1, waiting for transfers between devices, on_device(): lax.psum(grad_normed, HEAD)  71.2 us
    psum x8, blocking collectives, over_axes(): x = lax.psum(x, axis)  60.9 us
    all_to_all x9, starting transfers between devices, from_everyone(): lax.all_to_all(jnp.broadcast_to(x[None], (length, *x.shape)), axis, 0, 0,...  58.3 us
    another operation x18, other arithmetic  22.8 us
    unnamed x432, local copies, waits for them, and re-layouts  22.5 us
    all_to_all x2, waiting for transfers between devices, on_device(): lax.all_to_all(normalized_lower, 'seq', split_axis=1, concat_axis=0, tile...  20.1 us
  transfers between devices with their start and end apart: 22, of which 17 were waited for; matrix products, arithmetic and copies ran while one was open for 20% of the time, Pallas kernels for 0%

commit v1 on v0

v1 whole, which is shorter than its diff:
```python
from types import SimpleNamespace

import jax
import jax.numpy as jnp
from jax import lax
from jax.experimental import pallas as pl
from jax.experimental.pallas import tpu as pltpu
from jax.sharding import PartitionSpec as P

EPS = 1e-05
MESH = pl.DeviceIdType.MESH
HI = lax.Precision.HIGHEST
F32 = jnp.float32
BF16 = jnp.bfloat16

T = 256
R = 16
E = T + R
D = 1536
INNER = 3072
C = 192
N = 128
NH = 16
NS = 8
X = D + 128


def dot(a, b, ca, cb, precise=False):
    return lax.dot_general(
        a,
        b,
        (((ca,), (cb,)), ((), ())),
        precision=HI if precise else None,
        preferred_element_type=F32,
    )


def halves(a):
    if a.dtype == BF16:
        return (a,)
    hi = a.astype(BF16)
    return hi, (a - hi.astype(F32)).astype(BF16)


def fine(a, b, ca, cb):
    total = None
    for i, p in enumerate(halves(a)):
        for j, q in enumerate(halves(b)):
            if i + j < 2:
                term = dot(p, q, ca, cb)
                total = term if total is None else total + term
    return total


def iota(shape, dim):
    return lax.broadcasted_iota(jnp.int32, shape, dim)


def spread(col):
    rows = col.shape[0]
    lane = iota((rows, 128), 1)
    parts = [jnp.broadcast_to(col[:, 64 + k : 65 + k], (rows, 128)) for k in range(3)]
    return jnp.concatenate(
        [jnp.where(lane < 64, parts[0], parts[1]), jnp.where(lane < 64, parts[2], 0.0)], axis=1
    )


def split2(col):
    hi = col.astype(BF16)
    return hi, (col - hi.astype(F32)).astype(BF16)


def scalar_lanes(col):
    hi, lo = split2(col)
    lane = iota((col.shape[0], 128), 1)
    return jnp.where(lane == 0, hi.astype(F32), jnp.where(lane == 1, lo.astype(F32), 0.0)).astype(
        BF16
    )


def pack3(row):
    return jnp.where(iota((R, 128), 0) == 0, row, 0.0)


def unpack3(block):
    return block[0:1, :]


def decay_rows(log_row):
    e = jnp.exp(log_row)
    return jnp.concatenate(
        [jnp.broadcast_to(e[:, 64 + k : 65 + k], (64, 128)) for k in range(3)], axis=0
    )


def vm(*shape, dtype=F32):
    return pltpu.VMEM(shape, dtype)


def half(*shape):
    return pltpu.VMEM(shape, BF16)


def sem(*shape):
    return pltpu.SemaphoreType.DMA(shape)


def chain_refs():
    return dict(
        As=vm(2, C + R, N),
        Ar=vm(2, C + R, N),
        AS=sem(2),
        AR=sem(2),
        Bs=vm(2, C + R, N),
        Br=vm(2, 4, C + R, N),
        BS=sem(2, 4),
        BR=sem(2, 4),
        Cs=vm(2, C + R, N),
        Cr=vm(2, C + R, N),
        CS=sem(2),
        CR=sem(2),
    )


def weight_refs(w):
    return dict(
        s=half(2, 2, 4, C, w),
        r=half(2, 4, C, w),
        c=half(2, 4, C, w),
        x=half(2, 4, C, w),
        S=sem(2),
        R=sem(2),
        U=sem(2, 4),
        V=sem(2, 4),
    )


def both(*shape):
    return dict(S=sem(*shape), R=sem(*shape))


SCRATCH = dict(
    hid=vm(T, D),
    halo=vm(R, D),
    og=vm(T, D),
    wc=half(2, D, 768),
    wo=half(2, 256, D),
    nx0=half(E, X),
    nx1=half(E, X),
    pj=vm(2, E, 768),
    pre=vm(2, T, 512),
    x=vm(2, T, 256),
    dtb=vm(2, T, 256),
    ecb=vm(2, T, 256),
    etb=vm(2, T, 256),
    yi=vm(2, T, 256),
    yn=vm(2, T, 256),
    v=vm(2, T, 256),
    xdt=vm(2, T, 256),
    xtail=vm(2, T, 256),
    bm=half(2, T, N),
    cm=half(2, T, N),
    seg=vm(2, 3, T, T),
    vw=vm(2, 3, T, T),
    dt=vm(2, T, 128),
    cum=vm(2, T, 128),
    hl=vm(2, 256, N),
    hin=vm(2, 256, N),
    gl=vm(2, 256, N),
    gn=vm(2, 256, N),
    acc=vm(C, N),
    fc=chain_refs(),
    bc=chain_refs(),
    op=half(2, T, X),
    opr=half(2, NH, R, X),
    opq=both(2, NH),
    urow=vm(R, D),
    agq=both(NH),
    hxS=sem(NH),
    hxR=sem(1),
    h0=both(1),
    scs=vm(2, 8, T),
    scr=vm(2, NH, 8, T),
    scq=both(2, NH),
    hos=vm(NH, R, 128),
    hoq=both(NH),
    gm=half(2, T, D),
    gmq=both(NH),
    ggn=vm(2, T, 256),
    gnb=half(2, T, 256),
    gp=vm(2, T + 2 * R, 512),
    ge=half(2, E, 768),
    gq=half(2, E, D),
    gqr=half(2, 2 * NH, R, D),
    gqq=both(2, NH),
    ghS=sem(2),
    ghR=sem(2, NH),
    grow=vm(R, D),
    ngp=vm(2, 8, D),
    fas=vm(NH, 24, 128),
    far=vm(NH, 24, 128),
    faq=both(NH),
    sm=vm(2, 8, 512),
    cbs=vm(2, 8, 256),
    cbr=vm(NH, 2, 8, 256),
    cbq=both(NH),
    smr=vm(NS, 2, 8, 512),
    smq=both(NS),
    ngs=vm(8, 128),
    ngr=vm(NS, 8, 128),
    ngq=both(NS),
    we=weight_refs(512),
    wl=weight_refs(256),
    gbt=vm(2, 256, 384),
    gbr=vm(NH, 2, R, 384),
    gbq=both(NH),
    gcs=half(NS, 2, R, 256),
    gcr=half(NS, 2, R, 256),
    gcq=both(NS),
    gds=half(2, R, 256),
    gdq=both(NH),
    loc=sem(6),
)
LEAVES, TREE = jax.tree.flatten(SCRATCH)


def kernel(hid_in, og_in, ng_ref, sp_ref, wc_in, wo_in, ho, gi, wout, bct, smo, ngo, *scratch):
    m = SimpleNamespace(
        **{
            k: SimpleNamespace(**v) if isinstance(v, dict) else v
            for k, v in jax.tree.unflatten(TREE, scratch).items()
        }
    )
    s = lax.axis_index("seq")
    h = lax.axis_index("head")
    z = s // 2
    c = s % 2
    finals = []

    def rdma(src, dst, ss, rs, dev):
        return pltpu.make_async_remote_copy(
            src_ref=src, dst_ref=dst, send_sem=ss, recv_sem=rs, device_id=dev, device_id_type=MESH
        )

    def every(lo, hi, f):
        def step(d, carry):
            f(d)
            return carry

        lax.fori_loop(lo, hi, step, 0)

    class Ring:
        def __init__(self, mk, size):
            self.mk, self.size = mk, size

        def start(self):
            every(1, self.size, lambda d: self.mk(d).start())
            finals.append(lambda: every(1, self.size, lambda d: self.mk(d).wait_send()))

        def wait(self):
            every(1, self.size, lambda d: self.mk(d).wait_recv())

    def head_ring(src, dst, q, lead=()):
        def mk(d):
            t = lax.rem(h + d, NH)
            return rdma(
                src(t), dst(h), q.S.at[(*lead, d)], q.R.at[(*lead, d)], (s, t)
            )

        return Ring(mk, NH)

    def seq_ring(src, dst, q, lead=()):
        def mk(d):
            t = lax.rem(s + d, NS)
            return rdma(
                src(t), dst(s), q.S.at[(*lead, d)], q.R.at[(*lead, d)], (t, h)
            )

        return Ring(mk, NS)

    class One:
        def __init__(self, mk, sends, receives):
            self.mk, self.sends, self.receives = mk, sends, receives

        def start(self):
            @pl.when(self.sends)
            def _():
                self.mk().start()

            def last():
                @pl.when(self.sends)
                def _():
                    self.mk().wait_send()

            finals.append(last)

        def wait(self):
            @pl.when(self.receives)
            def _():
                self.mk().wait_recv()

    def rows16(t, base=0):
        return pl.ds(pl.multiple_of(base + t * R, R), R)

    loads = [
        pltpu.make_async_copy(hid_in, m.hid, m.loc.at[0]),
        pltpu.make_async_copy(wc_in.at[0], m.wc.at[0], m.loc.at[1]),
        pltpu.make_async_copy(wo_in.at[0], m.wo.at[0, pl.ds(0, C)], m.loc.at[2]),
        pltpu.make_async_copy(wc_in.at[1], m.wc.at[1], m.loc.at[3]),
        pltpu.make_async_copy(wo_in.at[1], m.wo.at[1, pl.ds(0, C)], m.loc.at[4]),
        pltpu.make_async_copy(og_in, m.og, m.loc.at[5]),
    ]
    for cp in loads:
        cp.start()

    bar = pltpu.get_barrier_semaphore()

    def greet(dev):
        pl.semaphore_signal(bar, inc=1, device_id=dev, device_id_type=MESH)

    every(1, NH, lambda d: greet((s, lax.rem(h + d, NH))))
    every(1, NS, lambda d: greet((lax.rem(s + d, NS), h)))
    back_halo = jnp.logical_and(s > 0, h < NH - 1)
    fore_halo = jnp.logical_and(s < NS - 1, h == NH - 1)

    @pl.when(back_halo)
    def _():
        greet((s - 1, NH - 1))

    @pl.when(fore_halo)
    def _():
        every(0, NH - 1, lambda t: greet((s + 1, t)))

    peers = NH - 1 + NS - 1 + jnp.where(back_halo, 1, 0) + jnp.where(fore_halo, NH - 1, 0)
    pl.semaphore_wait(bar, peers)

    halo0 = One(
        lambda: rdma(hid_in.at[pl.ds(T - R, R)], m.halo, m.h0.S.at[0], m.h0.R.at[0], (s + 1, h)),
        s < NS - 1,
        s > 0,
    )
    halo0.start()

    for l in range(2):
        m.wo[l, C:, :] = jnp.zeros((256 - C, D), BF16)

    def norm_rows(u, l):
        q = lax.rsqrt(jnp.mean(u * u, axis=1, keepdims=True) + EPS)
        return q, (u * q * ng_ref[l : l + 1, :]).astype(BF16)

    loads[0].wait()

    def norm_step(i):
        u = m.hid[pl.ds(pl.multiple_of(i * 32, 32), 32), :]
        m.nx0[pl.ds(pl.multiple_of(R + i * 32, R), 32), 0:D] = norm_rows(u, 0)[1]

    every(0, T // 32, norm_step)
    halo0.wait()

    @pl.when(s > 0)
    def _():
        m.nx0[0:R, 0:D] = norm_rows(m.halo[...], 0)[1]

    @pl.when(s == 0)
    def _():
        m.nx0[0:R, 0:D] = jnp.zeros((R, D), BF16)
        m.nx1[0:R, :] = jnp.zeros((R, X), BF16)

    nx = (m.nx0, m.nx1)
    lane = iota((T, 128), 1)
    dt_lane = jnp.logical_and(lane >= 64, lane < 67)
    lane256 = iota((T, 256), 1)
    head_lane = [jnp.logical_and(lane256 >= 64 * k, lane256 < 64 * k + 64) for k in range(3)]
    causal = iota((T, T), 0) >= iota((T, T), 1)
    tri = jnp.where(causal, 1.0, 0.0)

    def only(k, a):
        return jnp.where(head_lane[k], a, jnp.zeros_like(a))

    def chain(l, local, out, q, near, far, step):
        ld = m.cum[l, T - 1 : T, :]
        ra, rb, rc = q.Ar, q.Br, q.Cr
        sa, sb, sc = q.As, q.Bs, q.Cs
        A = One(
            lambda: rdma(sa.at[l], ra.at[l], q.AS.at[l], q.AR.at[l], (2 * z + near, h)),
            c == far,
            c == near,
        )

        def link(d):
            zz = z + step * d
            inside = jnp.logical_and(zz >= 0, zz < 4)
            prev = z - step * d
            gets = jnp.logical_and(prev >= 0, prev < 4)
            return One(
                lambda: rdma(
                    sb.at[l], rb.at[l, z], q.BS.at[l, d], q.BR.at[l, d], (2 * zz + near, h)
                ),
                jnp.logical_and(c == near, inside),
                jnp.logical_and(c == near, gets),
            )

        B = [link(d) for d in (1, 2, 3)]
        first = z == 0 if step > 0 else z == 3
        more = jnp.logical_not(first)
        Cc = One(
            lambda: rdma(sc.at[l], rc.at[l], q.CS.at[l], q.CR.at[l], (2 * z + far, h)),
            jnp.logical_and(c == near, more),
            jnp.logical_and(c == far, more),
        )

        def begin():
            @pl.when(c == far)
            def _():
                sa[l, 0:C, :] = local[l, 0:C, :]
                sa[l, C:, :] = pack3(ld)

            A.start()

        def middle():
            A.wait()

            @pl.when(c == near)
            def _():
                other = ra[l, 0:C, :].astype(F32)
                lo = unpack3(ra[l, C:, :])
                sb[l, 0:C, :] = (decay_rows(ld) * other + local[l, 0:C, :])
                sb[l, C:, :] = pack3(lo + ld)

            for b in B:
                b.start()

        def end():
            for b in B:
                b.wait()

            @pl.when(c == near)
            def _():
                m.acc[...] = jnp.zeros((C, N), F32)
                order = (0, 1, 2) if step > 0 else (3, 2, 1)
                for zz in order:

                    @pl.when(zz < z if step > 0 else zz > z)
                    def _():
                        m.acc[...] = decay_rows(unpack3(rb[l, zz, C:, :])) * m.acc[...] + rb[
                            l, zz, 0:C, :
                        ].astype(F32)

                sc[l, 0:C, :] = m.acc[...]
                sc[l, C:, :] = jnp.zeros((R, N), F32)

            Cc.start()
            out[l, C:, :] = jnp.zeros((256 - C, N), F32)

            @pl.when(c == near)
            def _():
                lo = unpack3(ra[l, C:, :])
                out[l, 0:C, :] = decay_rows(lo) * m.acc[...] + ra[l, 0:C, :].astype(F32)

            Cc.wait()

            @pl.when(c == far)
            def _():
                @pl.when(more)
                def _():
                    out[l, 0:C, :] = rc[l, 0:C, :].astype(F32)

                @pl.when(first)
                def _():
                    out[l, 0:C, :] = jnp.zeros((C, N), F32)

        return begin, middle, end

    def forward(l):
        for j in range(3):
            m.pj[l, :, 256 * j : 256 * j + 256] = dot(
                nx[l][:, 0:D], m.wc[l, :, 256 * j : 256 * j + 256], 1, 0
            )
        for pc, kc in ((0, 0), (512, 256)):
            a = sp_ref[l, 4:5, kc : kc + 256]
            for k in range(4):
                a = a + sp_ref[l, k : k + 1, kc : kc + 256] * m.pj[l, 13 + k : 13 + k + T, pc : pc + 256]
            m.pre[l, :, kc : kc + 256] = a
        a = m.pre[l, :, 0:256]
        x = a * jax.nn.sigmoid(a)
        m.x[l] = x
        a = m.pre[l, :, 256:512]
        bc = (a * jax.nn.sigmoid(a)).astype(BF16)
        m.bm[l] = bc[:, 0:N]
        m.cm[l] = bc[:, N:]
        a = m.pj[l, R:, 128:256] + sp_ref[l, 6:7, 0:128]
        dt = jnp.where(dt_lane, jax.nn.softplus(a), 0.0)
        la = -dt * jnp.exp(sp_ref[l, 7:8, 0:128])
        cum = dot(tri, la, 1, 0, True)
        m.dt[l] = dt
        m.cum[l] = cum
        dtb = spread(dt)
        etb = spread(jnp.exp(cum[T - 1 : T, :] - cum))
        m.dtb[l] = dtb
        m.etb[l] = etb
        m.ecb[l] = spread(jnp.exp(cum))
        m.xdt[l] = dtb * x
        m.xtail[l] = dtb * etb * x
        m.hl[l] = fine(m.xtail[l], m.bm[l], 0, 0)
        begin, middle, end = chain(l, m.hl, m.hin, m.fc, 1, 0, 1)
        begin()
        cumt = jnp.transpose(cum)
        scores = dot(m.cm[l], m.bm[l], 1, 1)
        for k in range(3):
            seg = jnp.where(
                causal, jnp.exp(cum[:, 64 + k : 65 + k] - cumt[64 + k : 65 + k, :]), 0.0
            )
            m.seg[l, k] = seg
            m.vw[l, k] = scores * seg
        middle()
        yi = jnp.zeros((T, 256), F32)
        for k in range(3):
            yi = yi + fine(m.vw[l, k], only(k, m.xdt[l]), 1, 0)
        m.yi[l] = yi
        end()
        yn = m.yi[l] + m.ecb[l] * fine(m.cm[l], m.hin[l], 1, 1)
        m.yn[l] = yn
        zz = m.pj[l, R:, 256:512]
        v = (yn + spread(sp_ref[l, 8:9, 0:128]) * m.x[l]) * (zz * jax.nn.sigmoid(zz))
        m.v[l] = v

    def mix_out(l):
        gain = sp_ref[l, 5:6, 0:256]
        v = m.v[l]
        vg = (v * gain).astype(BF16)
        for j in range(3):
            m.op[l, :, 512 * j : 512 * j + 512] = dot(
                vg, m.wo[l, :, 512 * j : 512 * j + 512], 1, 0
            ).astype(BF16)
        m.op[l, :, D:] = scalar_lanes(jnp.sum(v * v, axis=1, keepdims=True))
        ring = head_ring(
            lambda t: m.op.at[l, rows16(t)], lambda me: m.opr.at[l, me], m.opq, (l,)
        )
        ring.start()
        m.opr[l, h] = m.op[l, rows16(h), :]
        return ring

    def mix_sum(l, ring):
        ring.wait()
        total = m.opr[l, 0].astype(F32)
        for t in range(1, NH):
            total = total + m.opr[l, t].astype(F32)
        r = lax.rsqrt((total[:, D : D + 1] + total[:, D + 1 : D + 2]) / INNER + EPS)
        return r, total[:, 0:D]

    def scalars(l):
        v = m.v[l]
        ones = jnp.full((8, 256), 1.0, F32)
        first = dot(ones, v * v, 1, 1, True)
        second = dot(ones, m.ggn[l] * (sp_ref[l, 5:6, 0:256] * v), 1, 1, True)
        m.scs[l] = jnp.where(iota((8, T), 0) == 0, first, second)
        ring = head_ring(lambda t: m.scs.at[l], lambda me: m.scr.at[l, me], m.scq, (l,))
        ring.start()
        m.scr[l, h] = m.scs[l]
        ring.wait()
        total = m.scr[l, 0]
        for t in range(1, NH):
            total = total + m.scr[l, t]
        return jnp.transpose(jnp.concatenate([total, jnp.zeros((120, T), F32)], axis=0))

    def g_gate(l):
        return dot(m.gm[l], m.wo[l], 1, 1)

    def weight_parts(q, l, parts):
        w = q.r.shape[-1]
        for k in range(4):
            at = 0
            for left, right in parts:
                piece = dot(left(k), right, 0, 0)
                wide = piece.shape[1]
                q.s[l, 0, k, :, at : at + wide] = piece[0:C].astype(BF16)
                q.s[l, 1, k, :, at : at + wide] = piece[C:].astype(BF16)
                at += wide
        yes = jnp.bool_(True)
        pair = One(
            lambda: rdma(
                q.s.at[l, 1 - c],
                q.r.at[l],
                q.S.at[l],
                q.R.at[l],
                (2 * z + 1 - c, h),
            ),
            yes,
            yes,
        )
        pair.start()

        def mk(d):
            t = lax.rem(z + d, 4)
            return rdma(
                q.c.at[l, t],
                q.x.at[l, z],
                q.U.at[l, d],
                q.V.at[l, d],
                (2 * t + c, h),
            )

        ring = Ring(mk, 4)

        def middle():
            pair.wait()
            for k in range(4):
                q.c[l, k] = (
                    q.s[l, c, k].astype(F32) + q.r[l, k].astype(F32)
                ).astype(BF16)
            ring.start()
            q.x[l, z] = q.c[l, z]

        def end(col):
            ring.wait()
            wout[l, :, col : col + w] = (
                q.x[l, 0].astype(F32)
                + q.x[l, 1].astype(F32)
                + q.x[l, 2].astype(F32)
                + q.x[l, 3].astype(F32)
            )

        return middle, end

    def backward(l, r, s2, between):
        gain = sp_ref[l, 5:6, 0:256]
        skip = spread(sp_ref[l, 8:9, 0:128])
        v = m.v[l]
        ggn = m.ggn[l]
        rv = r * v
        m.sm[l, 5:6, 0:256] = jnp.sum(ggn * rv, axis=0, keepdims=True)
        m.gnb[l] = (rv * gain).astype(BF16)
        gv = r * (gain * ggn) - v * (r * r * r * s2 / INNER)
        zz = m.pj[l, R:, 256:512]
        sz = jax.nn.sigmoid(zz)
        x = m.x[l]
        y = m.yn[l] + skip * x
        m.ge[l, 0:R, 256:512] = jnp.zeros((R, 256), BF16)
        m.ge[l, R:, 256:512] = (gv * y * (sz * (1.0 + zz * (1.0 - sz)))).astype(BF16)
        gy = gv * (zz * sz)
        ecb = m.ecb[l]
        gyc = ecb * gy
        m.gl[l] = fine(gyc, m.cm[l], 0, 0)
        begin, middle, end = chain(l, m.gl, m.gn, m.bc, 0, 1, -1)
        begin()
        gxd = jnp.zeros((T, 256), F32)
        ds = jnp.zeros((T, T), F32)
        xdt = m.xdt[l]
        for k in range(3):
            g_k = only(k, gy)
            gxd = gxd + fine(m.vw[l, k], g_k, 0, 0)
            ds = ds + fine(g_k, xdt, 1, 1) * m.seg[l, k]
        middle()
        hin = m.hin[l]
        bm, cm = m.bm[l], m.cm[l]
        db = fine(ds, cm, 0, 0)
        dc = fine(ds, bm, 1, 0) + fine(gyc, hin, 1, 0)
        ecol = iota((256, 128), 0) // 64 + 64 == iota((256, 128), 1)
        ecol = jnp.where(jnp.logical_and(ecol, iota((256, 128), 0) < C), 1.0, 0.0)
        dcum = dot(gy * m.yn[l], ecol, 1, 0, True)
        col_in = dot(xdt * gxd, ecol, 1, 0, True)
        gskip = jnp.sum(dot(gy * x, ecol, 1, 0, True), axis=0, keepdims=True)
        between()
        end()
        gnx = m.gn[l]
        db = db + fine(m.xtail[l], gnx, 1, 0)
        rt = m.etb[l] * fine(bm, gnx, 1, 1)
        gxs = gxd + rt
        dtb = m.dtb[l]
        gx = dtb * gxs + skip * gy
        dt = m.dt[l]
        tail = dot(x * rt, ecol, 1, 0, True)
        gdt = dot(x * gxs, ecol, 1, 0, True)
        tail = dt * tail
        cum = m.cum[l]
        both = jnp.sum(gnx * m.hin[l], axis=1, keepdims=True)
        both = jnp.sum(both * ecol, axis=0, keepdims=True)
        last = jnp.sum(tail, axis=0, keepdims=True) + jnp.exp(cum[T - 1 : T, :]) * both
        dcum = dcum - col_in - tail + jnp.where(iota((T, 128), 0) == T - 1, last, 0.0)
        gla = dot(tri, dcum, 0, 0, True)
        rate = jnp.exp(sp_ref[l, 7:8, 0:128])
        gd = gdt - gla * rate
        a = m.pj[l, R:, 128:256] + sp_ref[l, 6:7, 0:128]
        gdtr = jnp.where(dt_lane, gd * jax.nn.sigmoid(a), 0.0)
        m.sm[l, 6:7, 0:128] = jnp.sum(gdtr, axis=0, keepdims=True)
        m.sm[l, 6:7, 128:256] = jnp.sum(-gla * dt * rate, axis=0, keepdims=True)
        m.sm[l, 6:7, 256:384] = gskip
        m.sm[l, 6:7, 384:512] = jnp.zeros((1, 128), F32)
        m.sm[l, 5:6, 256:512] = jnp.zeros((1, 256), F32)
        m.sm[l, 7:8, :] = jnp.zeros((1, 512), F32)
        for kc, gpost in ((0, gx), (256, jnp.concatenate([db, dc], axis=1))):
            a = m.pre[l, :, kc : kc + 256]
            sa = jax.nn.sigmoid(a)
            gpre = gpost * (sa * (1.0 + a * (1.0 - sa)))
            m.gp[l, 0:R, kc : kc + 256] = jnp.zeros((R, 256), F32)
            m.gp[l, R : R + T, kc : kc + 256] = gpre
            m.gp[l, R + T :, kc : kc + 256] = jnp.zeros((R, 256), F32)
            pc = 2 * kc
            for k in range(4):
                m.sm[l, k : k + 1, kc : kc + 256] = jnp.sum(
                    gpre * m.pj[l, 13 + k : 13 + k + T, pc : pc + 256], axis=0, keepdims=True
                )
            m.sm[l, 4:5, kc : kc + 256] = jnp.sum(gpre, axis=0, keepdims=True)
            gj = jnp.zeros((E, 256), F32)
            for k in range(4):
                gj = gj + sp_ref[l, k : k + 1, kc : kc + 256] * m.gp[l, 3 - k : 3 - k + E, kc : kc + 256]
            if kc == 0:
                more = jnp.concatenate([jnp.zeros((R, 128), F32), gdtr], axis=0)
                gj = gj + jnp.concatenate([jnp.zeros((E, 128), F32), more], axis=1)
            else:
                gt = jnp.transpose(jnp.concatenate([gj, jnp.zeros((384 - E, 256), F32)], axis=0))
                m.gbt[l] = gt
            m.ge[l, :, pc : pc + 256] = gj.astype(BF16)
        for j in range(3):
            m.gq[l, :, 512 * j : 512 * j + 512] = dot(
                m.ge[l], m.wc[l, 512 * j : 512 * j + 512, :], 1, 1
            ).astype(BF16)
        ring = head_ring(
            lambda t: m.gq.at[l, rows16(t, R)], lambda me: m.gqr.at[l, me], m.gqq, (l,)
        )
        ring.start()

        def mk(t):
            return rdma(
                m.gq.at[l, pl.ds(0, R)], m.gqr.at[l, NH + h], m.ghS.at[l], m.ghR.at[l, h], (s - 1, NH - 1)
            )

        halo = One(lambda: mk(0), s > 0, jnp.bool_(False))
        halo.start()
        m.gqr[l, h] = m.gq[l, rows16(h, R), :]

        def finish():
            ring.wait()
            total = m.gqr[l, 0].astype(F32)
            for t in range(1, NH):
                total = total + m.gqr[l, t].astype(F32)
            m.grow[...] = total

            @pl.when(fore_halo)
            def _():
                def wait_one(t):
                    rdma(
                        m.gq.at[l, pl.ds(0, R)], m.gqr.at[l, NH + t], m.ghS.at[l], m.ghR.at[l, t], (s + 1, 0)
                    ).wait_recv()

                every(0, NH, wait_one)
                more = m.gqr[l, NH].astype(F32)
                for t in range(1, NH):
                    more = more + m.gqr[l, NH + t].astype(F32)
                m.grow[...] = m.grow[...] + more

            return m.grow[...]

        return finish

    def norm_back(l, u, g, gn):
        q = lax.rsqrt(jnp.mean(u * u, axis=1, keepdims=True) + EPS)
        w = gn * ng_ref[l : l + 1, :]
        m.ngp[l, 0:1, :] = jnp.sum(gn * u * q, axis=0, keepdims=True)
        return g + q * w - u * (q * q * q * (jnp.sum(w * u, axis=1, keepdims=True) / D))

    loads[1].wait()
    forward(0)
    loads[2].wait()
    ring = mix_out(0)
    r0, o0 = mix_sum(0, ring)
    u1 = m.hid[rows16(h), :] + r0 * o0
    m.urow[...] = u1
    m.nx1[rows16(h, R), 0:D] = norm_rows(u1, 1)[1]
    m.nx1[rows16(h, R), D:] = scalar_lanes(r0)
    ag = head_ring(
        lambda t: m.nx1.at[rows16(h, R)], lambda me: m.nx1.at[rows16(me, R)], m.agq
    )
    ag.start()

    def halo1(t):
        return rdma(
            m.nx1.at[rows16(NH - 1, R)], m.nx1.at[pl.ds(0, R)], m.hxS.at[t], m.hxR.at[0], (s + 1, t)
        )

    @pl.when(fore_halo)
    def _():
        every(0, NH, lambda t: halo1(t).start())

    def halo1_sent():
        @pl.when(fore_halo)
        def _():
            every(0, NH, lambda t: halo1(t).wait_send())

    finals.append(halo1_sent)

    for cp in loads[3:]:
        cp.wait()
    m.gm[1] = m.og[...].astype(BF16)
    m.ggn[1] = g_gate(1)
    ag.wait()

    @pl.when(s > 0)
    def _():
        halo1(0).wait_recv()

    forward(1)
    cols = scalars(1)
    r1 = lax.rsqrt(cols[:, 0:1] / INNER + EPS)
    ring1 = mix_out(1)
    back1 = backward(1, r1, cols[:, 1:2], lambda: None)

    def left_n(l):
        return lambda k: nx[l][:, 384 * k : 384 * k + 384]

    def left_g(l):
        return lambda k: m.gm[l, :, 384 * k : 384 * k + 384]

    e1_mid, e1_end = weight_parts(
        m.we, 1, [(left_n(1), m.ge[1, :, 256:512]), (left_g(1), m.gnb[1])]
    )
    l1_mid, l1_end = weight_parts(m.wl, 1, [(left_n(1), m.ge[1, :, 0:256])])
    g_rows = norm_back(1, m.urow[...], m.og[rows16(h), :], back1())
    m.grow[...] = g_rows
    m.gm[0, rows16(h), :] = g_rows.astype(BF16)
    agm = head_ring(
        lambda t: m.gm.at[0, rows16(h)], lambda me: m.gm.at[0, rows16(me)], m.gmq
    )
    agm.start()

    e1_mid()
    l1_mid()
    rr, oo = mix_sum(1, ring1)
    final = m.urow[...] + rr * oo
    for t in range(NH):
        m.hos[t, :, 0:96] = final[:, 96 * t : 96 * t + 96]
        m.hos[t, :, 96:128] = jnp.zeros((R, 32), F32)
    hor = head_ring(lambda t: m.hos.at[t], lambda me: ho.at[rows16(me)], m.hoq)
    hor.start()
    ho[rows16(h), :] = m.hos[h]
    agm.wait()

    m.ggn[0] = g_gate(0)
    ex = m.nx1[R:, D:].astype(F32)
    cols = scalars(0)
    u_kept = m.grow[...]
    m.urow[...] = u_kept

    def between():
        e1_end(256)
        l1_end(0)

    back0 = backward(0, ex[:, 0:1] + ex[:, 1:2], cols[:, 1:2], between)

    gbr = head_ring(lambda t: m.gbt.at[:, rows16(t)], lambda me: m.gbr.at[me], m.gbq)
    gbr.start()
    m.gbr[h] = m.gbt[:, rows16(h), :]
    for l in range(2):
        m.cbs[l] = m.sm[l, :, 256:512]
    cbr = head_ring(lambda t: m.cbs, lambda me: m.cbr.at[me], m.cbq)
    cbr.start()
    m.cbr[h] = m.cbs[...]
    l0_mid, l0_end = weight_parts(m.wl, 0, [(left_n(0), m.ge[0, :, 0:256])])
    e0_mid, e0_end = weight_parts(
        m.we, 0, [(left_n(0), m.ge[0, :, 256:512]), (left_g(0), m.gnb[0])]
    )
    l0_mid()
    e0_mid()
    gbr.wait()
    for l in range(2):
        total = m.gbr[0, l].astype(F32)
        for t in range(1, NH):
            total = total + m.gbr[t, l].astype(F32)
        part = dot(total.astype(BF16)[:, 0:E], nx[l][:, 0:D], 1, 0).astype(BF16)
        for t in range(NS):
            m.gcs[t, l, :, 0:C] = part[:, C * t : C * t + C]
            m.gcs[t, l, :, C:] = jnp.zeros((R, 256 - C), BF16)
    gcr = seq_ring(lambda t: m.gcs.at[t], lambda me: m.gcr.at[me], m.gcq)
    gcr.start()
    m.gcr[s] = m.gcs[s]
    cbr.wait()
    total = m.cbr[0]
    for t in range(1, NH):
        total = total + m.cbr[t]
    for l in range(2):
        keep = iota((8, 256), 0) < 5
        m.sm[l, :, 256:512] = jnp.where(keep, total[l], m.sm[l, :, 256:512])
    smr = seq_ring(lambda t: m.sm, lambda me: m.smr.at[me], m.smq)
    smr.start()
    m.smr[s] = m.sm[...]
    gcr.wait()
    total = m.gcr[0].astype(F32)
    for t in range(1, NS):
        total = total + m.gcr[t].astype(F32)
    m.gds[...] = total.astype(BF16)
    gdr = head_ring(lambda t: m.gds, lambda me: bct.at[me], m.gdq)
    gdr.start()
    bct[h] = m.gds[...]
    g_rows = norm_back(0, m.hid[rows16(h), :], m.urow[...], back0())
    for t in range(NH):
        m.fas[t, 0:R, 0:96] = g_rows[:, 96 * t : 96 * t + 96]
        m.fas[t, 0:R, 96:128] = jnp.zeros((R, 32), F32)
        m.fas[t, R:, :] = jnp.zeros((8, 128), F32)
        for l in range(2):
            m.fas[t, R + l : R + l + 1, 0:96] = m.ngp[l, 0:1, 96 * t : 96 * t + 96]
    far = head_ring(lambda t: m.fas.at[t], lambda me: m.far.at[me], m.faq)
    far.start()
    m.far[h] = m.fas[h]
    l0_end(0)
    e0_end(256)
    smr.wait()
    total = m.smr[0]
    for t in range(1, NS):
        total = total + m.smr[t]
    smo[...] = total
    far.wait()
    total = m.far[0, R:, :]
    for t in range(1, NH):
        total = total + m.far[t, R:, :]
    m.ngs[...] = total
    ngr = seq_ring(lambda t: m.ngs, lambda me: m.ngr.at[me], m.ngq)
    ngr.start()
    m.ngr[s] = m.ngs[...]
    for t in range(NH):
        gi[R * t : R * t + R, :] = m.far[t, 0:R, :]
    gdr.wait()
    hor.wait()
    ngr.wait()
    total = m.ngr[0]
    for t in range(1, NS):
        total = total + m.ngr[t]
    ngo[...] = total
    for f in finals:
        f()


def on_device(
    hidden_in,
    norm_gain,
    gate_mixer_weight,
    w_bc,
    w_dt,
    conv_x,
    conv_bc,
    head_params,
    gate_gain,
    w_out,
    out_grad,
):
    def wide(a, before, total):
        pads = [(0, 0)] * (a.ndim - 1) + [(before, total - before - a.shape[-1])]
        return jnp.pad(a, pads)

    wc = jnp.concatenate(
        [
            wide(jnp.concatenate([gate_mixer_weight[:, :, 1], w_dt], axis=-1), 0, 256),
            wide(gate_mixer_weight[:, :, 0], 0, 256),
            w_bc,
        ],
        axis=-1,
    )
    sp = jnp.concatenate(
        [
            jnp.concatenate([wide(conv_x, 0, 256), conv_bc], axis=-1),
            wide(gate_gain[:, None, :], 0, 512),
            wide(head_params, 64, 512),
            jnp.zeros((2, 7, 512), F32),
        ],
        axis=1,
    )
    whole = pl.BlockSpec(memory_space=pltpu.VMEM)
    there = pl.BlockSpec(memory_space=pl.ANY)
    ho, gi, w, bct, smo, ngo = pl.pallas_call(
        kernel,
        out_shape=[
            jax.ShapeDtypeStruct((T, 128), F32),
            jax.ShapeDtypeStruct((T, 128), F32),
            jax.ShapeDtypeStruct((2, C, 768), F32),
            jax.ShapeDtypeStruct((NH, 2, R, 256), BF16),
            jax.ShapeDtypeStruct((2, 8, 512), F32),
            jax.ShapeDtypeStruct((8, 128), F32),
        ],
        in_specs=[there, there, whole, whole, there, there],
        out_specs=[whole] * 6,
        scratch_shapes=LEAVES,
        compiler_params=pltpu.CompilerParams(
            collective_id=0, has_side_effects=True, vmem_limit_bytes=60 * 2**20
        ),
        name="two_layers",
    )(hidden_in, out_grad, norm_gain, sp, wc, w_out)
    w_bc_grad = jnp.transpose(bct, (1, 3, 0, 2)).reshape(2, 256, 256)[:, :C].astype(F32)
    heads = jnp.stack([smo[:, 6, 64:67], smo[:, 6, 192:195], smo[:, 6, 320:323]], axis=1)
    return (
        ho[:, :96],
        gi[:, :96],
        ngo[0:2, :96],
        jnp.stack([w[:, :, 256:448], w[:, :, 0:192]], axis=2),
        w_bc_grad,
        w[:, :, 192:195],
        smo[:, 0:5, 0:192],
        smo[:, 0:5, 256:512],
        heads,
        smo[:, 5, 0:192],
        jnp.transpose(w[:, :, 512:704], (0, 2, 1)),
    )


def solution(mesh):
    return jax.shard_map(
        on_device,
        mesh=mesh,
        in_specs=(
            P("seq", None),
            P(),
            P(None, None, None, "head"),
            P(),
            P(None, None, "head"),
            P(None, None, "head"),
            P(),
            P(None, None, "head"),
            P(None, "head"),
            P(None, "head", None),
            P("seq", None),
        ),
        out_specs=(
            P("seq", "head"),
            P("seq", "head"),
            P(None, "head"),
            P(None, "seq", None, "head"),
            P(None, "seq", None),
            P(None, "seq", "head"),
            P(None, None, "head"),
            P(),
            P(None, None, "head"),
            P(None, "head"),
            P(None, "head", "seq"),
        ),
        check_vma=False,
    )
```

time: 786 us -> 205 us (0.26); the launches traced: 773 us -> 204 us
  waiting for transfers between devices: 333 us -> 0 us
  Pallas kernels: 0 us -> 178 us
  local copies, waits for them, and re-layouts: 111 us -> 18.9 us
  starting transfers between devices: 91.9 us -> 0 us
  other arithmetic: 92.6 us -> 6.48 us
  matrix products: 67.5 us -> 0 us
  blocking collectives: 60.9 us -> 0 us
  between operations: 16.9 us -> 0.83 us
    pallas_call x0 -> x1, Pallas kernels: none -> 178 us  [on_device(): pl.pallas_call(kernel, out_shape=[jax.ShapeDtypeStruct((T, 128), F32), ja...]
    all_to_all x13 -> x0, waiting for transfers between devices: 160 us -> none  [the longest x9 128 us: from_everyone(): lax.all_to_all(jnp.broadcast_to(x[None], (length, *x.shape)), axis, 0, 0,...]
    psum x3 -> x0, waiting for transfers between devices: 155 us -> none  [the longest x2 83.8 us: on_device(): residual = residual + lax.psum(mixer_term, HEAD)]
    all_to_all x13 -> x0, starting transfers between devices: 77.4 us -> none  [the longest x9 58.3 us: from_everyone(): lax.all_to_all(jnp.broadcast_to(x[None], (length, *x.shape)), axis, 0, 0,...]
    dot_general x50 -> x0, matrix products: 64.9 us -> none  [the longest x6 11.4 us: block_scan(): jnp.einsum('hts,hsp->htp', weights, jnp.transpose(inputs, (1, 0, 2)), pre...]
    psum x8 -> x0, blocking collectives: 60.9 us -> none  [over_axes(): x = lax.psum(x, axis)]
    reduce_sum x19 -> x0, other arithmetic: 30 us -> none  [the longest x3 11.2 us: over_copies(): return from_everyone(x, axis).sum(axis=0)]
    another operation x31 -> x2, other arithmetic: 27.8 us -> 0.07 us  [the longest x1 0.05 us: on_device(): jnp.stack([w[:, :, 256:448], w[:, :, 0:192]], axis=2)]
  transfers between devices with their start and end apart: 22 -> 0, of which waited for: 17 -> 0; matrix products, arithmetic and copies ran while one was open for 20% -> 0% of each run, Pallas kernels for 0% -> 0%
where the time goes in v1:
time: 205 us; the launch traced here: 204 us
  Pallas kernels  178 us (87%)
  local copies, waits for them, and re-layouts  18.9 us (9%)
  other arithmetic  6.48 us (3%)
    pallas_call x1, Pallas kernels, on_device(): pl.pallas_call(kernel, out_shape=[jax.ShapeDtypeStruct((T, 128), F32), ja...  178 us
    unnamed x34, local copies, waits for them, and re-layouts  11.5 us

profile of v1, /device:TPU:1, one launch (start us, length us, event | category | flops | bytes accessed | tf_op | source)
XLA Modules:
  0.0 204.4 jit_solution(18375374104639174467)
XLA Ops:
  0.6 2.9 %fusion.11 = (bf16[2,1536,1,192]{1,3,2,0:T(8,128)(2,1)S(1)}, bf16[2,1536,1,192]{1,3,2,0:T(8,128)(2,1)}) fusion(bf16[2,1536,2,192]{1,3,2,0:T(8,128)(2,1)} %param.13), kind=kLoop, calls=%fused_computation.30 | loop fusion | bytes 4718592 | tf_op jit(solution)/shard_map/slice | solution.py:951
  3.5 0.7 copy.53
  4.2 1.2 copy.40
  5.5 1.7 fusion.6
  7.2 1.6 copy.54
  8.9 3.9 %fusion.3.wc_in = bf16[2,1536,768]{2,1,0:T(8,128)(2,1)} fusion(bf16[2,1536,192]{2,1,0:T(8,128)(2,1)S(1)} %bitcast.15, bf16[2,1536,256]{2,1,0:T(8,128)(2,1)} %param.14, bf16[2,1536,256]{2,1,0:T(8,128)(2,1)S(1)} %fusion.6), kind=kLoop, calls=%fused_computation.5 | loop fusion | flops 23592960 | bytes 9043968 | tf_op jit(solution)/shard_map/concatenate | solution.py:949
  12.9 0.1 pad.39.clone
  13.0 0.7 fusion.7.sp_ref
  13.7 178.2 %two_layers.1 = (f32[256,128]{1,0:T(8,128)}, f32[256,128]{1,0:T(8,128)}, f32[2,192,768]{2,1,0:T(8,128)}, bf16[16,2,16,256]{3,2,1,0:T(8,128)(2,1)}, f32[2,8,512]{2,1,0:T(8,128)}, /*index=5*/f32[8,128]{1,0:T(8,128)}) custom-call(f32[256,1536]{1,0:T(8,128)} %hid_in.1, f32[256,1536]{1,0:T(8,128)} %og_in.1, f32[2,1536]{1,0:T(2,128)} %ng_ref.1, ...), custom_call_target="tpu_custom_call" | custom-call | tf_op jit(solution)/shard_map/two_layers/pallas_call | solution.py:968
  191.9 0.8 fusion.12
  192.7 0.6 copy.50
  193.3 1.3 slice_bitcast_fusion
  194.7 0.1 pad_maximum_fusion
  194.8 1.5 copy.45
  196.2 0.9 copy.51
  197.2 0.6 copy.48
  197.8 0.6 copy.49
  198.4 0.6 copy.56
  199.0 1.0 slice.56
  200.0 0.7 copy.47
  200.8 0.9 copy.46
  201.7 0.7 copy.43
  202.5 0.7 copy.44
  203.2 1.2 slice.52
  (29 shorter events, 0.2 us)
Async XLA Ops:
  3.5 0.7 copy-start.4
  8.8 4.0 %copy-start.5 = (f32[2,5,192]{2,0,1:T(2,128)S(1)}, f32[2,5,192]{2,0,1:T(2,128)}, u32[]{:S(2)}) copy-start(f32[2,5,192]{2,0,1:T(2,128)} %param.16) | copy-start | bytes 23044
  8.8 4.0 %copy-start.6 = (f32[2,5,256]{2,0,1:T(2,128)S(1)}, f32[2,5,256]{2,0,1:T(2,128)}, u32[]{:S(2)}) copy-start(f32[2,5,256]{2,0,1:T(2,128)} %param.17) | copy-start | bytes 30724
  8.9 4.0 %copy-start.7 = (f32[2,3,3]{2,0,1:T(2,128)S(1)}, f32[2,3,3]{2,0,1:T(2,128)}, u32[]{:S(2)}) copy-start(f32[2,3,3]{2,0,1:T(2,128)} %param.18) | copy-start | bytes 220
  8.9 4.0 %copy-start.8 = (f32[2,192]{1,0:T(2,128)S(1)}, f32[2,192]{1,0:T(2,128)}, u32[]{:S(2)}) copy-start(f32[2,192]{1,0:T(2,128)} %param.19) | copy-start | bytes 4612
  194.7 2.5 %copy-start.3 = (f32[2,8,512]{2,1,0:T(8,128)S(1)}, f32[2,8,512]{2,1,0:T(8,128)}, u32[]{:S(2)}) copy-start(f32[2,8,512]{2,1,0:T(8,128)} %get-tuple-element.22) | copy-start | bytes 98308
  194.7 6.1 %copy-start = (bf16[16,2,16,256]{3,2,1,0:T(8,128)(2,1)S(1)}, bf16[16,2,16,256]{3,2,1,0:T(8,128)(2,1)}, u32[]{:S(2)}) copy-start(bf16[16,2,16,256]{3,2,1,0:T(8,128)(2,1)} %get-tuple-element.21) | copy-start | bytes 786436
  194.7 7.0 %copy-start.2 = (f32[256,128]{1,0:T(8,128)S(1)}, f32[256,128]{1,0:T(8,128)}, u32[]{:S(2)}) copy-start(f32[256,128]{1,0:T(8,128)} %get-tuple-element.17) | copy-start | bytes 393220
  196.2 6.2 %copy-start.1 = (f32[256,128]{1,0:T(8,128)S(1)}, f32[256,128]{1,0:T(8,128)}, u32[]{:S(2)}) copy-start(f32[256,128]{1,0:T(8,128)} %get-tuple-element.18) | copy-start | bytes 393220

commit v2 on v1

v2 whole, which is shorter than its diff:
```python
from types import SimpleNamespace

import jax
import jax.numpy as jnp
from jax import lax
from jax.experimental import pallas as pl
from jax.experimental.pallas import tpu as pltpu
from jax.sharding import PartitionSpec as P

EPS = 1e-05
MESH = pl.DeviceIdType.MESH
HI = lax.Precision.HIGHEST
F32 = jnp.float32
BF16 = jnp.bfloat16

T = 256
R = 16
G = 8
D = 1536
INNER = 3072
C = 192
N = 128
NH = 16
NS = 8
X = D + 128
S = D // NH


def dot(a, b, ca, cb, precise=False):
    return lax.dot_general(
        a,
        b,
        (((ca,), (cb,)), ((), ())),
        precision=HI if precise else None,
        preferred_element_type=F32,
    )


def halves(a):
    if a.dtype == BF16:
        return (a,)
    hi = a.astype(BF16)
    return hi, (a - hi.astype(F32)).astype(BF16)


def fine(a, b, ca, cb):
    total = None
    for i, p in enumerate(halves(a)):
        for j, q in enumerate(halves(b)):
            if i + j < 2:
                term = dot(p, q, ca, cb)
                total = term if total is None else total + term
    return total


def iota(shape, dim):
    return lax.broadcasted_iota(jnp.int32, shape, dim)


def padded(a, lanes=256):
    return jnp.concatenate([a, jnp.zeros((a.shape[0], lanes - a.shape[1]), a.dtype)], axis=1)


def spread(col):
    rows = col.shape[0]
    lane = iota((rows, 128), 1)
    parts = [jnp.broadcast_to(col[:, k : k + 1], (rows, 128)) for k in range(3)]
    return jnp.concatenate(
        [jnp.where(lane < 64, parts[0], parts[1]), jnp.where(lane < 64, parts[2], 0.0)], axis=1
    )


def scalar_lanes(col):
    hi = col.astype(BF16).astype(F32)
    lane = iota((col.shape[0], 128), 1)
    return jnp.where(lane == 0, hi, jnp.where(lane == 1, col - hi, 0.0)).astype(BF16)


def decay_rows(log_row):
    e = jnp.exp(log_row)
    return jnp.concatenate(
        [jnp.broadcast_to(e[:, k : k + 1], (64, 128)) for k in range(3)], axis=0
    )


def vm(*shape, dtype=F32):
    return pltpu.VMEM(shape, dtype)


def half(*shape):
    return pltpu.VMEM(shape, BF16)


def sem(*shape):
    return pltpu.SemaphoreType.DMA(shape)


def both(*shape):
    return dict(S=sem(*shape), R=sem(*shape))


def chain_refs():
    return dict(
        As=vm(2, C + G, N),
        Ar=vm(2, C + G, N),
        AS=sem(2),
        AR=sem(2),
        Bs=vm(2, C + G, N),
        Br=vm(2, 4, C + G, N),
        BS=sem(2, 4),
        BR=sem(2, 4),
        Cs=vm(2, C, N),
        Cr=vm(2, C, N),
        CS=sem(2),
        CR=sem(2),
    )


def weight_refs(w):
    return dict(
        s=half(2, 2, 4, C, w),
        r=half(2, 4, C, w),
        c=half(2, 4, C, w),
        x=half(2, 4, C, w),
        S=sem(2),
        R=sem(2),
        U=sem(2, 4),
        V=sem(2, 4),
    )


SCRATCH = dict(
    hid=vm(T, D),
    og=vm(T, D),
    wz=half(2, 2, C, D),
    wb=half(2, D, 256),
    wo=half(2, C, D),
    sp=vm(2, 16, 512),
    q0=vm(T, 128),
    nx0=half(T, D),
    nx1=half(T, X),
    pj=vm(2, G + T, 768),
    pre=vm(2, T, 512),
    pjd=vm(2, T, 128),
    jhS=sem(2),
    jhR=sem(2),
    x=vm(2, T, 256),
    dtb=vm(2, T, 256),
    ecb=vm(2, T, 256),
    etb=vm(2, T, 256),
    yn=vm(2, T, 256),
    v=vm(2, T, 256),
    xdt=vm(2, T, 256),
    xtail=vm(2, T, 256),
    bm=half(2, T, N),
    cm=half(2, T, N),
    seg=vm(2, 3, T, T),
    vw=vm(2, 3, T, T),
    dt=vm(2, T, 128),
    cum=vm(2, T, 128),
    hl=vm(2, 256, N),
    hin=vm(2, 256, N),
    gl=vm(2, 256, N),
    gn=vm(2, 256, N),
    acc=vm(C, N),
    fc=chain_refs(),
    bc=chain_refs(),
    op=half(2, T, X),
    opr=half(2, NH, R, X),
    opq=both(2, NH),
    urow=vm(R, D),
    agq=both(NH),
    scs=vm(2, 8, T),
    scr=vm(2, NH, 8, T),
    scq=both(2, NH),
    hos=vm(NH, R, 128),
    hoq=both(NH),
    gm=half(2, T, D),
    gmq=both(NH),
    ggn=vm(2, T, 256),
    gnb=half(2, T, 256),
    gp=vm(2, T + G, 512),
    ghS=sem(2),
    ghR=sem(2),
    ge=half(2, T, 768),
    gq=half(2, T, D),
    gqr=half(2, NH, R, D),
    gqq=both(2, NH),
    grow=vm(R, D),
    ngp=vm(2, 8, D),
    fas=vm(NH, R, 128),
    faq=both(NH),
    sm=vm(2, 8, 512),
    gbs=vm(2, NH, R + G, 256),
    gbr=vm(2, NH, R + G, 256),
    gbq=both(2, NH),
    smr=vm(2, NS, 8, 512),
    smq=both(2, NS),
    gcs=half(2, NS, R, 256),
    gcr=half(2, NS, R, 256),
    gcq=both(2, NS),
    gds=half(2, R, 256),
    gdq=both(2, NH),
    we=weight_refs(512),
    wl=weight_refs(256),
    loc=sem(8),
)
LEAVES, TREE = jax.tree.flatten(SCRATCH)


def kernel(
    hid_in,
    og_in,
    ng_ref,
    cx_ref,
    cb_ref,
    hp_ref,
    gg_ref,
    wd_ref,
    wz_in,
    wb_in,
    wo_in,
    ho,
    gi,
    wout,
    bct,
    smo,
    *scratch,
):
    m = SimpleNamespace(
        **{
            k: SimpleNamespace(**v) if isinstance(v, dict) else v
            for k, v in jax.tree.unflatten(TREE, scratch).items()
        }
    )
    s = lax.axis_index("seq")
    h = lax.axis_index("head")
    z = s // 2
    c = s % 2
    finals = []

    def rdma(src, dst, ss, rs, dev):
        return pltpu.make_async_remote_copy(
            src_ref=src, dst_ref=dst, send_sem=ss, recv_sem=rs, device_id=dev, device_id_type=MESH
        )

    def every(lo, hi, f):
        def step(d, carry):
            f(d)
            return carry

        lax.fori_loop(lo, hi, step, 0)

    class Ring:
        def __init__(self, mk, size):
            self.mk, self.size = mk, size

        def start(self):
            every(1, self.size, lambda d: self.mk(d).start())
            finals.append(lambda: every(1, self.size, lambda d: self.mk(d).wait_send()))

        def wait(self):
            every(1, self.size, lambda d: self.mk(d).wait_recv())

    def head_ring(src, dst, q, lead=()):
        def mk(d):
            t = lax.rem(h + d, NH)
            return rdma(src(t), dst(h), q.S.at[(*lead, d)], q.R.at[(*lead, d)], (s, t))

        return Ring(mk, NH)

    def seq_ring(src, dst, q, lead=()):
        def mk(d):
            t = lax.rem(s + d, NS)
            return rdma(src(t), dst(s), q.S.at[(*lead, d)], q.R.at[(*lead, d)], (t, h))

        return Ring(mk, NS)

    class One:
        def __init__(self, mk, sends, receives):
            self.mk, self.sends, self.receives = mk, sends, receives

        def start(self):
            @pl.when(self.sends)
            def _():
                self.mk().start()

            def last():
                @pl.when(self.sends)
                def _():
                    self.mk().wait_send()

            finals.append(last)

        def wait(self):
            @pl.when(self.receives)
            def _():
                self.mk().wait_recv()

    def rows16(t):
        return pl.ds(pl.multiple_of(t * R, R), R)

    loads = [
        pltpu.make_async_copy(hid_in, m.hid, m.loc.at[0]),
        pltpu.make_async_copy(wz_in.at[0], m.wz.at[0], m.loc.at[1]),
        pltpu.make_async_copy(wb_in.at[0], m.wb.at[0], m.loc.at[2]),
        pltpu.make_async_copy(wo_in.at[0], m.wo.at[0], m.loc.at[3]),
        pltpu.make_async_copy(wz_in.at[1], m.wz.at[1], m.loc.at[4]),
        pltpu.make_async_copy(wb_in.at[1], m.wb.at[1], m.loc.at[5]),
        pltpu.make_async_copy(wo_in.at[1], m.wo.at[1], m.loc.at[6]),
        pltpu.make_async_copy(og_in, m.og, m.loc.at[7]),
    ]
    for cp in loads:
        cp.start()

    bar = pltpu.get_barrier_semaphore()

    def greet(dev):
        pl.semaphore_signal(bar, inc=1, device_id=dev, device_id_type=MESH)

    every(1, NS, lambda d: greet((lax.rem(s + d, NS), h)))
    every(1, NH, lambda d: greet((s, lax.rem(h + d, NH))))

    m.sp[...] = jnp.zeros((2, 16, 512), F32)
    for l in range(2):
        for k in range(5):
            m.sp[l, k : k + 1, 0:C] = cx_ref[k, l : l + 1, :]
            m.sp[l, k : k + 1, 256:512] = cb_ref[k, l : l + 1, :]
        m.sp[l, 5:6, 0:C] = gg_ref[l : l + 1, :]
        for k in range(3):
            m.sp[l, 6 + k : 7 + k, 0:3] = hp_ref[k, l : l + 1, :]
    sp = m.sp

    def norm_rows(u, l):
        q = lax.rsqrt(jnp.mean(u * u, axis=1, keepdims=True) + EPS)
        return q, (u * q * ng_ref[l : l + 1, :]).astype(BF16)

    loads[0].wait()

    def norm_step(i):
        at = pl.ds(pl.multiple_of(i * 32, 32), 32)
        q, n = norm_rows(m.hid[at, :], 0)
        m.nx0[at, :] = n
        m.q0[at, :] = jnp.broadcast_to(q, (32, 128))

    every(0, T // 32, norm_step)

    nx = (m.nx0, m.nx1)
    lane = iota((T, 128), 1)
    dt_lane = lane < 3
    lane256 = iota((T, 256), 1)
    head_lane = [jnp.logical_and(lane256 >= 64 * k, lane256 < 64 * k + 64) for k in range(3)]
    causal = iota((T, T), 0) >= iota((T, T), 1)
    tri = jnp.where(causal, 1.0, 0.0)
    ecol = jnp.where(iota((256, 128), 0) // 64 == iota((256, 128), 1), 1.0, 0.0)
    ecol = jnp.where(iota((256, 128), 1) < 3, ecol, 0.0)

    def only(k, a):
        return jnp.where(head_lane[k], a, jnp.zeros_like(a))

    def silu_slope(a):
        sa = jax.nn.sigmoid(a)
        return sa * (1.0 + a * (1.0 - sa))

    def chain(l, local, out, q, near, far, step):
        ld = m.cum[l, T - 1 : T, :]
        ra, rb, rc = q.Ar, q.Br, q.Cr
        sa, sb, sc = q.As, q.Bs, q.Cs
        A = One(
            lambda: rdma(sa.at[l], ra.at[l], q.AS.at[l], q.AR.at[l], (2 * z + near, h)),
            c == far,
            c == near,
        )

        def link(d):
            zz = z + step * d
            inside = jnp.logical_and(zz >= 0, zz < 4)
            prev = z - step * d
            gets = jnp.logical_and(prev >= 0, prev < 4)
            return One(
                lambda: rdma(
                    sb.at[l], rb.at[l, z], q.BS.at[l, d], q.BR.at[l, d], (2 * zz + near, h)
                ),
                jnp.logical_and(c == near, inside),
                jnp.logical_and(c == near, gets),
            )

        B = [link(d) for d in (1, 2, 3)]
        first = z == 0 if step > 0 else z == 3
        more = jnp.logical_not(first)
        Cc = One(
            lambda: rdma(sc.at[l], rc.at[l], q.CS.at[l], q.CR.at[l], (2 * z + far, h)),
            jnp.logical_and(c == near, more),
            jnp.logical_and(c == far, more),
        )

        def begin():
            @pl.when(c == far)
            def _():
                sa[l, 0:C, :] = local[l, 0:C, :]
                sa[l, C:, :] = jnp.broadcast_to(ld, (G, N))

            A.start()

        def middle():
            A.wait()

            @pl.when(c == near)
            def _():
                other = ra[l, 0:C, :]
                lo = ra[l, C : C + 1, :]
                sb[l, 0:C, :] = decay_rows(ld) * other + local[l, 0:C, :]
                sb[l, C:, :] = jnp.broadcast_to(lo + ld, (G, N))

            for b in B:
                b.start()

        def end():
            for b in B:
                b.wait()

            @pl.when(c == near)
            def _():
                m.acc[...] = jnp.zeros((C, N), F32)
                order = (0, 1, 2) if step > 0 else (3, 2, 1)
                for zz in order:

                    @pl.when(zz < z if step > 0 else zz > z)
                    def _():
                        m.acc[...] = decay_rows(rb[l, zz, C : C + 1, :]) * m.acc[...] + rb[
                            l, zz, 0:C, :
                        ]

                sc[l] = m.acc[...]

            Cc.start()
            out[l, C:, :] = jnp.zeros((256 - C, N), F32)

            @pl.when(c == near)
            def _():
                lo = ra[l, C : C + 1, :]
                out[l, 0:C, :] = decay_rows(lo) * m.acc[...] + ra[l, 0:C, :]

            Cc.wait()

            @pl.when(c == far)
            def _():
                @pl.when(more)
                def _():
                    out[l, 0:C, :] = rc[l]

                @pl.when(first)
                def _():
                    out[l, 0:C, :] = jnp.zeros((C, N), F32)

        return begin, middle, end

    def forward(l, ready):
        n = nx[l][:, 0:D]
        m.pj[l, G:, 0:256] = padded(dot(n, m.wz[l, 1], 1, 1))
        m.pj[l, G:, 256:512] = dot(n, m.wb[l], 1, 0)
        ready()
        halo = One(
            lambda: rdma(
                m.pj.at[l, pl.ds(T, G), pl.ds(0, 512)],
                m.pj.at[l, pl.ds(0, G), pl.ds(0, 512)],
                m.jhS.at[l],
                m.jhR.at[l],
                (s + 1, h),
            ),
            s < NS - 1,
            s > 0,
        )
        halo.start()
        m.pjd[l] = padded(dot(n, wd_ref[l], 1, 1), 128)
        m.pj[l, G:, 512:768] = padded(dot(n, m.wz[l, 0], 1, 1))
        dt = jnp.where(dt_lane, jax.nn.softplus(m.pjd[l] + sp[l, 6:7, 0:128]), 0.0)
        la = -dt * jnp.exp(sp[l, 7:8, 0:128])
        cum = dot(tri, la, 1, 0, True)
        m.dt[l] = dt
        m.cum[l] = cum
        dtb = spread(dt)
        etb = spread(jnp.exp(cum[T - 1 : T, :] - cum))
        m.dtb[l] = dtb
        m.etb[l] = etb
        m.ecb[l] = spread(jnp.exp(cum))
        cumt = jnp.transpose(cum)
        for k in range(3):
            m.seg[l, k] = jnp.where(causal, jnp.exp(cum[:, k : k + 1] - cumt[k : k + 1, :]), 0.0)

        @pl.when(s == 0)
        def _():
            m.pj[l, 0:G, 0:512] = jnp.zeros((G, 512), F32)

        halo.wait()
        for kc in (256, 0):
            a = sp[l, 4:5, kc : kc + 256]
            for k in range(4):
                at = G - 3 + k
                a = a + sp[l, k : k + 1, kc : kc + 256] * m.pj[l, at : at + T, kc : kc + 256]
            m.pre[l, :, kc : kc + 256] = a
            post = a * jax.nn.sigmoid(a)
            if kc:
                m.bm[l] = post[:, 0:N].astype(BF16)
                m.cm[l] = post[:, N:].astype(BF16)
        x = post
        m.x[l] = x
        m.xdt[l] = dtb * x
        m.xtail[l] = dtb * etb * x
        m.hl[l] = fine(m.xtail[l], m.bm[l], 0, 0)
        begin, middle, end = chain(l, m.hl, m.hin, m.fc, 1, 0, 1)
        begin()
        scores = dot(m.cm[l], m.bm[l], 1, 1)
        for k in range(3):
            m.vw[l, k] = scores * m.seg[l, k]
        middle()
        yi = jnp.zeros((T, 256), F32)
        for k in range(3):
            yi = yi + fine(m.vw[l, k], only(k, m.xdt[l]), 1, 0)
        m.yn[l] = yi
        end()
        yn = m.yn[l] + m.ecb[l] * fine(m.cm[l], m.hin[l], 1, 1)
        m.yn[l] = yn
        zz = m.pj[l, G:, 512:768]
        m.v[l] = (yn + spread(sp[l, 8:9, 0:128]) * m.x[l]) * (zz * jax.nn.sigmoid(zz))

    def mix_out(l):
        v = m.v[l]
        vg = (v * sp[l, 5:6, 0:256])[:, 0:C].astype(BF16)
        for j in range(3):
            at = slice(512 * j, 512 * j + 512)
            m.op[l, :, at] = dot(vg, m.wo[l, :, at], 1, 0).astype(BF16)
        m.op[l, :, D:] = scalar_lanes(jnp.sum(v * v, axis=1, keepdims=True))
        ring = head_ring(
            lambda t: m.op.at[l, rows16(t)], lambda me: m.opr.at[l, me], m.opq, (l,)
        )
        ring.start()
        m.opr[l, h] = m.op[l, rows16(h), :]
        return ring

    def total_of(ref, count):
        total = ref[0].astype(F32)
        for t in range(1, count):
            total = total + ref[t].astype(F32)
        return total

    def mix_sum(l, ring):
        ring.wait()
        total = total_of(m.opr.at[l], NH)
        r = lax.rsqrt((total[:, D : D + 1] + total[:, D + 1 : D + 2]) / INNER + EPS)
        return r, total[:, 0:D]

    def scalars(l):
        v = m.v[l]
        ones = jnp.full((8, 256), 1.0, F32)
        first = dot(ones, v * v, 1, 1, True)
        second = dot(ones, m.ggn[l] * (sp[l, 5:6, 0:256] * v), 1, 1, True)
        m.scs[l] = jnp.where(iota((8, T), 0) == 0, first, second)
        ring = head_ring(lambda t: m.scs.at[l], lambda me: m.scr.at[l, me], m.scq, (l,))
        ring.start()
        m.scr[l, h] = m.scs[l]

        def end():
            ring.wait()
            total = total_of(m.scr.at[l], NH)
            return jnp.transpose(jnp.concatenate([total, jnp.zeros((120, T), F32)], axis=0))

        return end

    def g_gate(l):
        m.ggn[l] = padded(dot(m.gm[l], m.wo[l], 1, 1))

    def weight_parts(q, l, parts):
        w = q.r.shape[-1]
        for k in range(4):
            at = 0
            for left, right in parts:
                piece = dot(left[:, 384 * k : 384 * k + 384], right, 0, 0)
                wide = piece.shape[1]
                q.s[l, 0, k, :, at : at + wide] = piece[0:C].astype(BF16)
                q.s[l, 1, k, :, at : at + wide] = piece[C:].astype(BF16)
                at += wide
        yes = jnp.bool_(True)
        pair = One(
            lambda: rdma(
                q.s.at[l, 1 - c], q.r.at[l], q.S.at[l], q.R.at[l], (2 * z + 1 - c, h)
            ),
            yes,
            yes,
        )
        pair.start()

        def mk(d):
            t = lax.rem(z + d, 4)
            return rdma(
                q.c.at[l, t], q.x.at[l, z], q.U.at[l, d], q.V.at[l, d], (2 * t + c, h)
            )

        ring = Ring(mk, 4)

        def middle():
            pair.wait()
            for k in range(4):
                q.c[l, k] = (q.s[l, c, k].astype(F32) + q.r[l, k].astype(F32)).astype(BF16)
            ring.start()
            q.x[l, z] = q.c[l, z]

        def end(col):
            ring.wait()
            wout[l, :, col : col + w] = total_of(q.x.at[l], 4)

        return middle, end

    def backward(l, r, s2, early, late):
        gain = sp[l, 5:6, 0:256]
        skip = spread(sp[l, 8:9, 0:128])
        v = m.v[l]
        ggn = m.ggn[l]
        rv = r * v
        gv = r * (gain * ggn) - v * (r * r * r * s2 / INNER)
        zz = m.pj[l, G:, 512:768]
        sz = jax.nn.sigmoid(zz)
        x = m.x[l]
        y = m.yn[l] + skip * x
        gy = gv * (zz * sz)
        gyc = m.ecb[l] * gy
        m.gl[l] = fine(gyc, m.cm[l], 0, 0)
        begin, middle, end = chain(l, m.gl, m.gn, m.bc, 0, 1, -1)
        begin()
        m.sm[l, 5:6, 0:256] = jnp.sum(ggn * rv, axis=0, keepdims=True)
        m.gnb[l] = (rv * gain).astype(BF16)
        m.ge[l, :, 512:768] = (gv * y * (sz * (1.0 + zz * (1.0 - sz)))).astype(BF16)
        gxd = jnp.zeros((T, 256), F32)
        ds = jnp.zeros((T, T), F32)
        xdt = m.xdt[l]
        for k in range(3):
            g_k = only(k, gy)
            gxd = gxd + fine(m.vw[l, k], g_k, 0, 0)
            ds = ds + fine(g_k, xdt, 1, 1) * m.seg[l, k]
        middle()
        weight_mid, weight_end = weight_parts(
            m.we, l, [(nx[l], m.ge[l, :, 512:768]), (m.gm.at[l], m.gnb[l])]
        )
        bm, cm = m.bm[l], m.cm[l]
        db = fine(ds, cm, 0, 0)
        dc = fine(ds, bm, 1, 0) + fine(gyc, m.hin[l], 1, 0)
        dcum = dot(gy * m.yn[l], ecol, 1, 0, True)
        col_in = dot(xdt * gxd, ecol, 1, 0, True)
        gskip = jnp.sum(dot(gy * x, ecol, 1, 0, True), axis=0, keepdims=True)
        early()
        end()
        weight_mid()
        gnx = m.gn[l]
        db = db + fine(m.xtail[l], gnx, 1, 0)
        rt = m.etb[l] * fine(bm, gnx, 1, 1)
        gxs = gxd + rt
        gx = m.dtb[l] * gxs + skip * gy
        for kc, gpost in ((0, gx), (256, jnp.concatenate([db, dc], axis=1))):
            gpre = gpost * silu_slope(m.pre[l, :, kc : kc + 256])
            m.gp[l, 0:T, kc : kc + 256] = gpre
        halo = One(
            lambda: rdma(
                m.gp.at[l, pl.ds(0, G)], m.gp.at[l, pl.ds(T, G)], m.ghS.at[l], m.ghR.at[l], (s - 1, h)
            ),
            s > 0,
            s < NS - 1,
        )
        halo.start()
        dt = m.dt[l]
        tail = dot(x * rt, ecol, 1, 0, True)
        gdt = dot(x * gxs, ecol, 1, 0, True)
        tail = dt * tail
        cum = m.cum[l]
        inner = jnp.sum(gnx * m.hin[l], axis=1, keepdims=True)
        inner = jnp.sum(inner * ecol, axis=0, keepdims=True)
        last = jnp.sum(tail, axis=0, keepdims=True) + jnp.exp(cum[T - 1 : T, :]) * inner
        dcum = dcum - col_in - tail + jnp.where(iota((T, 128), 0) == T - 1, last, 0.0)
        gla = dot(tri, dcum, 0, 0, True)
        rate = jnp.exp(sp[l, 7:8, 0:128])
        gd = gdt - gla * rate
        gdtr = jnp.where(dt_lane, gd * jax.nn.sigmoid(m.pjd[l] + sp[l, 6:7, 0:128]), 0.0)
        m.sm[l, 5:6, 256:512] = jnp.zeros((1, 256), F32)
        m.sm[l, 6:7, 0:128] = jnp.sum(gdtr, axis=0, keepdims=True)
        m.sm[l, 6:7, 128:256] = jnp.sum(-gla * dt * rate, axis=0, keepdims=True)
        m.sm[l, 6:7, 256:384] = gskip
        m.sm[l, 6:7, 384:512] = jnp.zeros((1, 128), F32)
        m.sm[l, 7:8, :] = jnp.zeros((1, 512), F32)
        for kc in (0, 256):
            gpre = m.gp[l, 0:T, kc : kc + 256]
            for k in range(4):
                at = G - 3 + k
                m.sm[l, k : k + 1, kc : kc + 256] = jnp.sum(
                    gpre * m.pj[l, at : at + T, kc : kc + 256], axis=0, keepdims=True
                )
            m.sm[l, 4:5, kc : kc + 256] = jnp.sum(gpre, axis=0, keepdims=True)

        @pl.when(s == NS - 1)
        def _():
            m.gp[l, T:, :] = jnp.zeros((G, 512), F32)

        halo.wait()
        for kc in (0, 256):
            gj = jnp.zeros((T, 256), F32)
            for k in range(4):
                gj = gj + sp[l, k : k + 1, kc : kc + 256] * m.gp[l, 3 - k : 3 - k + T, kc : kc + 256]
            if kc == 0:
                gj = jnp.concatenate([gj[:, 0:C], gdtr[:, 0:64]], axis=1)
            else:
                gt = jnp.transpose(gj)
                for t in range(NH):
                    m.gbs[l, t, 0:R, :] = gt[R * t : R * t + R, :]
            m.ge[l, :, kc : kc + 256] = gj.astype(BF16)
        low = gdtr[:, 0:R].astype(BF16)
        for j in range(3):
            at = slice(512 * j, 512 * j + 512)
            part = (
                dot(m.ge[l, :, 0:C], m.wz[l, 1, :, at], 1, 0)
                + dot(m.ge[l, :, 512 : 512 + C], m.wz[l, 0, :, at], 1, 0)
                + dot(m.ge[l, :, 256:512], m.wb[l, at, :], 1, 1)
                + dot(low, wd_ref[l, :, at], 1, 0)
            )
            if l == 0:
                m.ngp[l, 0:1, at] = jnp.sum(part * (m.hid[:, at] * m.q0[:, 0:1]), axis=0, keepdims=True)
            m.gq[l, :, at] = part.astype(BF16)
        ring = head_ring(
            lambda t: m.gq.at[l, rows16(t)], lambda me: m.gqr.at[l, me], m.gqq, (l,)
        )
        ring.start()
        m.gqr[l, h] = m.gq[l, rows16(h), :]
        late()
        last_mid, last_end = weight_parts(m.wl, l, [(nx[l], m.ge[l, :, 0:256])])

        def finish():
            ring.wait()
            return total_of(m.gqr.at[l], NH)

        return finish, weight_end, last_mid, last_end

    def norm_back(l, u, g, gn):
        q = lax.rsqrt(jnp.mean(u * u, axis=1, keepdims=True) + EPS)
        w = gn * ng_ref[l : l + 1, :]
        if l:
            m.ngp[l, 0:1, :] = jnp.sum(gn * u * q, axis=0, keepdims=True)
        return g + q * w - u * (q * q * q * (jnp.sum(w * u, axis=1, keepdims=True) / D))

    class Small:
        def __init__(self, l):
            self.l = l
            self.a = head_ring(
                lambda t: m.gbs.at[l, t], lambda me: m.gbr.at[l, me], m.gbq, (l,)
            )
            self.b = seq_ring(lambda t: m.gcs.at[l, t], lambda me: m.gcr.at[l, me], m.gcq, (l,))
            self.c = seq_ring(lambda t: m.sm.at[l], lambda me: m.smr.at[l, me], m.smq, (l,))
            self.d = head_ring(lambda t: m.gds.at[l], lambda me: bct.at[l, me], m.gdq, (l,))

        def first(self):
            l = self.l
            for t in range(NH):
                m.gbs[l, t, R : R + 5, :] = m.sm[l, 0:5, 256:512]
                m.gbs[l, t, R + 5 : R + 6, 0:S] = m.ngp[l, 0:1, S * t : S * t + S]
                m.gbs[l, t, R + 5 : R + 6, S:] = jnp.zeros((1, 256 - S), F32)
                m.gbs[l, t, R + 6 :, :] = jnp.zeros((2, 256), F32)
            self.a.start()
            m.gbr[l, h] = m.gbs[l, h]

        def second(self):
            l = self.l
            self.a.wait()
            total = total_of(m.gbr.at[l], NH)
            m.sm[l, 0:5, 256:512] = total[R : R + 5]
            m.sm[l, 7:8, 0:256] = total[R + 5 : R + 6]
            part = dot(total[0:R].astype(BF16), nx[l][:, 0:D], 1, 0).astype(BF16)
            for t in range(NS):
                m.gcs[l, t] = padded(part[:, C * t : C * t + C])
            self.b.start()
            self.c.start()
            m.gcr[l, s] = m.gcs[l, s]
            m.smr[l, s] = m.sm[l]

        def third(self):
            l = self.l
            self.b.wait()
            m.gds[l] = total_of(m.gcr.at[l], NS).astype(BF16)
            self.d.start()
            bct[l, h] = m.gds[l]
            self.c.wait()
            smo[l] = total_of(m.smr.at[l], NS)

    small = [Small(0), Small(1)]

    loads[1].wait()
    loads[2].wait()
    forward(0, lambda: pl.semaphore_wait(bar, NH - 1 + NS - 1))
    loads[3].wait()
    r0, o0 = mix_sum(0, mix_out(0))
    u1 = m.hid[rows16(h), :] + r0 * o0
    m.urow[...] = u1
    m.nx1[rows16(h), 0:D] = norm_rows(u1, 1)[1]
    m.nx1[rows16(h), D:] = scalar_lanes(r0)
    ag = head_ring(lambda t: m.nx1.at[rows16(h)], lambda me: m.nx1.at[rows16(me)], m.agq)
    ag.start()

    for cp in loads[4:]:
        cp.wait()
    m.gm[1] = m.og[...].astype(BF16)
    g_gate(1)
    ag.wait()

    forward(1, lambda: None)
    cols = scalars(1)()
    r1 = lax.rsqrt(cols[:, 0:1] / INNER + EPS)
    rings = []

    def hidden_rows():
        rr, oo = mix_sum(1, rings[0])
        final = m.urow[...] + rr * oo
        for t in range(NH):
            m.hos[t] = padded(final[:, S * t : S * t + S], 128)

    back1, e1_end, l1_mid, l1_end = backward(
        1, r1, cols[:, 1:2], lambda: rings.append(mix_out(1)), lambda: None
    )
    l1_mid()
    hidden_rows()
    g_rows = norm_back(1, m.urow[...], m.og[rows16(h), :], back1())
    m.grow[...] = g_rows
    m.gm[0, rows16(h), :] = g_rows.astype(BF16)
    agm = head_ring(
        lambda t: m.gm.at[0, rows16(h)], lambda me: m.gm.at[0, rows16(me)], m.gmq
    )
    agm.start()
    ex = m.nx1[:, D:].astype(F32)
    r0 = ex[:, 0:1] + ex[:, 1:2]
    e1_end(256)
    l1_end(0)
    agm.wait()

    g_gate(0)
    cols = scalars(0)()
    hor = head_ring(lambda t: m.hos.at[t], lambda me: ho.at[rows16(me)], m.hoq)

    def early0():
        hor.start()
        ho[rows16(h), :] = m.hos[h]
        small[1].first()

    back0, e0_end, l0_mid, l0_end = backward(0, r0, cols[:, 1:2], early0, small[0].first)
    small[1].second()
    small[0].second()
    l0_mid()
    small[1].third()
    g_rows = norm_back(0, m.hid[rows16(h), :], m.grow[...], back0())
    for t in range(NH):
        m.fas[t] = padded(g_rows[:, S * t : S * t + S], 128)
    far = head_ring(lambda t: m.fas.at[t], lambda me: gi.at[rows16(me)], m.faq)
    far.start()
    gi[rows16(h), :] = m.fas[h]
    small[0].third()
    e0_end(256)
    l0_end(0)
    hor.wait()
    small[1].d.wait()
    small[0].d.wait()
    far.wait()
    for f in finals:
        f()


def arrange(ho, gi, w, bct, smo, o_ho, o_gi, o_ng, o_zx, o_bc, o_dt, o_cx, o_cb, o_hp, o_gg, o_wo):
    o_ho[...] = jnp.transpose(ho[...])[0:S, :]
    o_gi[...] = jnp.transpose(gi[...])[0:S, :]
    for l in range(2):
        o_ng[l : l + 1, :] = smo[l, 7:8, 0:S]
        o_zx[l, :, 0, :] = w[l, :, 256 : 256 + C]
        o_zx[l, :, 1, :] = w[l, :, 0:C]
        rows = jnp.concatenate([bct[l, t].astype(F32) for t in range(NH)], axis=0)
        o_bc[l] = jnp.transpose(rows)[0:C, :]
        dts = jnp.transpose(w[l, :, 128:256])
        for k in range(3):
            o_dt[k, l : l + 1, :] = dts[64 + k : 65 + k, :]
            o_hp[k, l : l + 1, :] = smo[l, 6:7, 128 * k : 128 * k + 3]
        for k in range(5):
            o_cx[k, l : l + 1, :] = smo[l, k : k + 1, 0:C]
            o_cb[k, l : l + 1, :] = smo[l, k : k + 1, 256:512]
        o_gg[l : l + 1, :] = smo[l, 5:6, 0:C]
        o_wo[l] = jnp.transpose(w[l, :, 512:768])[0:C, :]


def on_device(
    hidden_in,
    norm_gain,
    gate_mixer_weight,
    w_bc,
    w_dt,
    conv_x,
    conv_bc,
    head_params,
    gate_gain,
    w_out,
    out_grad,
):
    wd = jnp.pad(jnp.transpose(w_dt, (0, 2, 1)), ((0, 0), (0, R - 3), (0, 0)))
    whole = pl.BlockSpec(memory_space=pltpu.VMEM)
    there = pl.BlockSpec(memory_space=pl.ANY)

    def out(*shape, dtype=F32):
        return jax.ShapeDtypeStruct(shape, dtype)

    raw = pl.pallas_call(
        kernel,
        out_shape=[
            out(T, 128),
            out(T, 128),
            out(2, C, 768),
            out(2, NH, R, 256, dtype=BF16),
            out(2, 8, 512),
        ],
        in_specs=[there] * 2 + [whole] * 6 + [there] * 3,
        out_specs=[whole] * 5,
        scratch_shapes=LEAVES,
        compiler_params=pltpu.CompilerParams(
            collective_id=0, has_side_effects=True, vmem_limit_bytes=60 * 2**20
        ),
        name="two_layers",
    )(
        hidden_in,
        out_grad,
        norm_gain,
        jnp.transpose(conv_x, (1, 0, 2)),
        jnp.transpose(conv_bc, (1, 0, 2)),
        jnp.transpose(head_params, (1, 0, 2)),
        gate_gain,
        wd,
        jnp.transpose(gate_mixer_weight, (0, 2, 3, 1)),
        w_bc,
        w_out,
    )
    ho, gi, ng, zx, bc, dt, cx, cb, hp, gg, wo = pl.pallas_call(
        arrange,
        out_shape=[
            out(S, T),
            out(S, T),
            out(2, S),
            out(2, C, 2, C),
            out(2, C, 256),
            out(3, 2, C),
            out(5, 2, C),
            out(5, 2, 256),
            out(3, 2, 3),
            out(2, C),
            out(2, C, C),
        ],
        in_specs=[whole] * 5,
        out_specs=[whole] * 11,
        compiler_params=pltpu.CompilerParams(vmem_limit_bytes=40 * 2**20),
        name="arrange",
    )(*raw)
    return (
        jnp.transpose(ho),
        jnp.transpose(gi),
        ng,
        zx,
        bc,
        jnp.transpose(dt, (1, 2, 0)),
        jnp.transpose(cx, (1, 0, 2)),
        jnp.transpose(cb, (1, 0, 2)),
        jnp.transpose(hp, (1, 0, 2)),
        gg,
        wo,
    )


def solution(mesh):
    return jax.shard_map(
        on_device,
        mesh=mesh,
        in_specs=(
            P("seq", None),
            P(),
            P(None, None, None, "head"),
            P(),
            P(None, None, "head"),
            P(None, None, "head"),
            P(),
            P(None, None, "head"),
            P(None, "head"),
            P(None, "head", None),
            P("seq", None),
        ),
        out_specs=(
            P("seq", "head"),
            P("seq", "head"),
            P(None, "head"),
            P(None, "seq", None, "head"),
            P(None, "seq", None),
            P(None, "seq", "head"),
            P(None, None, "head"),
            P(),
            P(None, None, "head"),
            P(None, "head"),
            P(None, "head", "seq"),
        ),
        check_vma=False,
    )
```

time: 205 us -> 156 us (0.76)
  Pallas kernels: 178 us -> 149 us
  local copies, waits for them, and re-layouts: 18.9 us -> 6.16 us
  other arithmetic: 6.48 us -> 0 us
    pallas_call x1 -> x2, Pallas kernels: 178 us -> 149 us  [the longest x1 147 us: on_device(): pl.pallas_call(kernel, out_shape=[out(T, 128), out(T, 128), out(2, C, 768...]
    concatenate x3 -> x0, other arithmetic: 6.37 us -> none  [the longest x1 3.94 us: on_device(): jnp.concatenate([wide(jnp.concatenate([gate_mixer_weight[:, :, 1], w_dt],...]
    unnamed x34 -> x11, local copies, waits for them, and re-layouts: 11.5 us -> 5.51 us
    slice x7 -> x0, local copies, waits for them, and re-layouts: 5.95 us -> none  [the longest x1 2.87 us: on_device(): gate_mixer_weight[:, :, 1]]
where the time goes in v2:
time: 156 us
  Pallas kernels  149 us (96%)
  local copies, waits for them, and re-layouts  6.16 us (4%)
    pallas_call x1, Pallas kernels, on_device(): pl.pallas_call(kernel, out_shape=[out(T, 128), out(T, 128), out(2, C, 768...  147 us
    unnamed x11, local copies, waits for them, and re-layouts  5.51 us

profile of v2, /device:TPU:1, one launch (start us, length us, event | category | flops | bytes accessed | tf_op | source)
XLA Modules:
  0.0 155.8 jit_solution(10675226596714233499)
XLA Ops:
  0.6 0.7 copy.24
  1.4 0.7 pad.4.wd_ref
  2.0 147.3 %two_layers.1 = (f32[256,128]{1,0:T(8,128)}, f32[256,128]{1,0:T(8,128)}, f32[2,192,768]{2,1,0:T(8,128)}, bf16[2,16,16,256]{3,2,1,0:T(8,128)(2,1)}, f32[2,8,512]{2,1,0:T(8,128)}) custom-call(f32[256,1536]{1,0:T(8,128)} %hid_in.1, f32[256,1536]{1,0:T(8,128)} %og_in.1, f32[2,1536]{1,0:T(2,128)} %ng_ref.1, f32[5,2,192]{2,1,0:T(2,128)} %bitcast.15, ...), custom_call_target="tpu_custom_call" | custom-call | tf_op jit(solution)/shard_map/two_layers/pallas_call | solution.py:909
  149.4 0.0 copy-start
  149.4 1.3 copy-done
  150.6 0.0 copy-start.1
  150.6 0.9 copy-done.1
  151.6 0.0 copy-start.2
  151.6 0.9 copy-done.2
  152.5 0.0 copy-start.3
  152.5 0.9 copy-done.3
  153.4 0.0 copy-start.4
  153.4 0.8 copy-done.4
  154.1 1.6 %arrange.1 = (f32[96,256]{1,0:T(8,128)}, f32[96,256]{1,0:T(8,128)}, f32[2,96]{1,0:T(2,128)}, f32[2,192,2,192]{3,2,1,0:T(2,128)}, f32[2,192,256]{2,1,0:T(8,128)},...) custom-call(f32[256,128]{1,0:T(8,128)S(1)} %copy-done.2, ...), custom_call_target="tpu_custom_call" | custom-call | tf_op jit(solution)/shard_map/arrange/pallas_call | solution.py:938
Async XLA Ops:
  149.4 1.3 copy-start
  150.6 0.9 copy-start.1
  151.6 0.9 copy-start.2
  152.5 0.9 copy-start.3
  153.4 0.8 copy-start.4

commit v3 on v2

--- a/solution.py
+++ b/solution.py
@@ -136,9 +136,10 @@
     wb=half(2, D, 256),
     wo=half(2, C, D),
     sp=vm(2, 16, 512),
+    wd=half(2, R, D),
     q0=vm(T, 128),
     nx0=half(T, D),
-    nx1=half(T, X),
+    nx1=half(T, D),
     pj=vm(2, G + T, 768),
     pre=vm(2, T, 512),
     pjd=vm(2, T, 128),
@@ -165,17 +166,25 @@
     acc=vm(C, N),
     fc=chain_refs(),
     bc=chain_refs(),
-    op=half(2, T, X),
-    opr=half(2, NH, R, X),
+    op0=vm(T, D),
+    opr0=vm(NH, R, D),
+    op1=half(T, D),
+    opr1=half(NH, R, D),
     opq=both(2, NH),
+    lo=half(T, D),
+    lor=half(NH, R, D),
+    loq=both(NH),
+    r0=vm(T, 128),
     urow=vm(R, D),
+    orow=vm(R, D),
     agq=both(NH),
-    scs=vm(2, 8, T),
-    scr=vm(2, NH, 8, T),
+    scs=vm(2, 8, 128),
+    scr=vm(2, NH, 8, 128),
     scq=both(2, NH),
     hos=vm(NH, R, 128),
     hoq=both(NH),
-    gm=half(2, T, D),
+    gm0=half(T, X),
+    gm1=half(T, D),
     gmq=both(NH),
     ggn=vm(2, T, 256),
     gnb=half(2, T, 256),
@@ -237,6 +246,8 @@
     h = lax.axis_index("head")
     z = s // 2
     c = s % 2
+    hx = h // 4
+    hy = h % 4
     finals = []
 
     def rdma(src, dst, ss, rs, dev):
@@ -252,29 +263,39 @@
         lax.fori_loop(lo, hi, step, 0)
 
     class Ring:
-        def __init__(self, mk, size):
-            self.mk, self.size = mk, size
+        def __init__(self, mk, size, send):
+            self.mk, self.size, self.send = mk, size, send
 
         def start(self):
-            every(1, self.size, lambda d: self.mk(d).start())
+            self.send(lambda d: self.mk(d).start())
             finals.append(lambda: every(1, self.size, lambda d: self.mk(d).wait_send()))
 
         def wait(self):
             every(1, self.size, lambda d: self.mk(d).wait_recv())
 
+    def far_first(f):
+        def step(i):
+            d = (6 - i // 4) % 4 * 4 + (6 - i % 4) % 4
+
+            @pl.when(d > 0)
+            def _():
+                f(d)
+
+        every(0, NH, step)
+
     def head_ring(src, dst, q, lead=()):
         def mk(d):
-            t = lax.rem(h + d, NH)
+            t = (hx + d // 4) % 4 * 4 + (hy + d % 4) % 4
             return rdma(src(t), dst(h), q.S.at[(*lead, d)], q.R.at[(*lead, d)], (s, t))
 
-        return Ring(mk, NH)
+        return Ring(mk, NH, far_first)
 
     def seq_ring(src, dst, q, lead=()):
         def mk(d):
             t = lax.rem(s + d, NS)
             return rdma(src(t), dst(s), q.S.at[(*lead, d)], q.R.at[(*lead, d)], (t, h))
 
-        return Ring(mk, NS)
+        return Ring(mk, NS, lambda f: every(1, NS, f))
 
     class One:
         def __init__(self, mk, sends, receives):
@@ -310,7 +331,7 @@
         pltpu.make_async_copy(wo_in.at[1], m.wo.at[1], m.loc.at[6]),
         pltpu.make_async_copy(og_in, m.og, m.loc.at[7]),
     ]
-    for cp in loads:
+    for cp in loads[:4]:
         cp.start()
 
     bar = pltpu.get_barrier_semaphore()
@@ -329,6 +350,8 @@
         m.sp[l, 5:6, 0:C] = gg_ref[l : l + 1, :]
         for k in range(3):
             m.sp[l, 6 + k : 7 + k, 0:3] = hp_ref[k, l : l + 1, :]
+        rows = [wd_ref[k, l : l + 1, :].astype(F32) for k in range(3)]
+        m.wd[l] = jnp.concatenate(rows + [jnp.zeros((R - 3, D), F32)], axis=0).astype(BF16)
     sp = m.sp
 
     def norm_rows(u, l):
@@ -346,6 +369,7 @@
     every(0, T // 32, norm_step)
 
     nx = (m.nx0, m.nx1)
+    gm = (m.gm0, m.gm1)
     lane = iota((T, 128), 1)
     dt_lane = lane < 3
     lane256 = iota((T, 256), 1)
@@ -456,7 +480,7 @@
         return begin, middle, end
 
     def forward(l, ready):
-        n = nx[l][:, 0:D]
+        n = nx[l][...]
         m.pj[l, G:, 0:256] = padded(dot(n, m.wz[l, 1], 1, 1))
         m.pj[l, G:, 256:512] = dot(n, m.wb[l], 1, 0)
         ready()
@@ -472,7 +496,10 @@
             s > 0,
         )
         halo.start()
-        m.pjd[l] = padded(dot(n, wd_ref[l], 1, 1), 128)
+        if l == 0:
+            for cp in loads[4:]:
+                cp.start()
+        m.pjd[l] = padded(dot(n, m.wd[l], 1, 1), 128)
         m.pj[l, G:, 512:768] = padded(dot(n, m.wz[l, 0], 1, 1))
         dt = jnp.where(dt_lane, jax.nn.softplus(m.pjd[l] + sp[l, 6:7, 0:128]), 0.0)
         la = -dt * jnp.exp(sp[l, 7:8, 0:128])
@@ -524,19 +551,25 @@
         zz = m.pj[l, G:, 512:768]
         m.v[l] = (yn + spread(sp[l, 8:9, 0:128]) * m.x[l]) * (zz * jax.nn.sigmoid(zz))
 
+    def gate_norm(l, r):
+        exact = r * m.v[l] * sp[l, 5:6, 0:256]
+        m.gnb[l] = exact.astype(BF16)
+        return exact - m.gnb[l].astype(F32)
+
     def mix_out(l):
-        v = m.v[l]
-        vg = (v * sp[l, 5:6, 0:256])[:, 0:C].astype(BF16)
+        op, opr = ((m.op0, m.opr0), (m.op1, m.opr1))[l]
         for j in range(3):
             at = slice(512 * j, 512 * j + 512)
-            m.op[l, :, at] = dot(vg, m.wo[l, :, at], 1, 0).astype(BF16)
-        m.op[l, :, D:] = scalar_lanes(jnp.sum(v * v, axis=1, keepdims=True))
-        ring = head_ring(
-            lambda t: m.op.at[l, rows16(t)], lambda me: m.opr.at[l, me], m.opq, (l,)
-        )
+            op[:, at] = dot(m.gnb[l, :, 0:C], m.wo[l, :, at], 1, 0).astype(op.dtype)
+        ring = head_ring(lambda t: op.at[rows16(t)], lambda me: opr.at[me], m.opq, (l,))
         ring.start()
-        m.opr[l, h] = m.op[l, rows16(h), :]
-        return ring
+        opr[h] = op[rows16(h), :]
+
+        def end():
+            ring.wait()
+            return total_of(opr, NH)
+
+        return end
 
     def total_of(ref, count):
         total = ref[0].astype(F32)
@@ -544,31 +577,28 @@
             total = total + ref[t].astype(F32)
         return total
 
-    def mix_sum(l, ring):
+    def scalars(i, *values):
+        ones = jnp.full((8, 256), 1.0, F32)
+        row = iota((8, 128), 0)
+        packed = jnp.zeros((8, 128), F32)
+        for k, value in enumerate(values):
+            sums = dot(ones, value, 1, 1, True)
+            packed = jnp.where(row == 2 * k, sums[:, 0:128], packed)
+            packed = jnp.where(row == 2 * k + 1, sums[:, 128:256], packed)
+        m.scs[i] = packed
+        ring = head_ring(lambda t: m.scs.at[i], lambda me: m.scr.at[i, me], m.scq, (i,))
+        ring.start()
+        m.scr[i, h] = m.scs[i]
         ring.wait()
-        total = total_of(m.opr.at[l], NH)
-        r = lax.rsqrt((total[:, D : D + 1] + total[:, D + 1 : D + 2]) / INNER + EPS)
-        return r, total[:, 0:D]
-
-    def scalars(l):
-        v = m.v[l]
-        ones = jnp.full((8, 256), 1.0, F32)
-        first = dot(ones, v * v, 1, 1, True)
-        second = dot(ones, m.ggn[l] * (sp[l, 5:6, 0:256] * v), 1, 1, True)
-        m.scs[l] = jnp.where(iota((8, T), 0) == 0, first, second)
-        ring = head_ring(lambda t: m.scs.at[l], lambda me: m.scr.at[l, me], m.scq, (l,))
-        ring.start()
-        m.scr[l, h] = m.scs[l]
-
-        def end():
-            ring.wait()
-            total = total_of(m.scr.at[l], NH)
-            return jnp.transpose(jnp.concatenate([total, jnp.zeros((120, T), F32)], axis=0))
-
-        return end
+        total = total_of(m.scr.at[i], NH)
+        cols = jnp.transpose(jnp.concatenate([total, jnp.zeros((120, 128), F32)], axis=0))
+        return [
+            jnp.concatenate([cols[:, 2 * k : 2 * k + 1], cols[:, 2 * k + 1 : 2 * k + 2]], axis=0)
+            for k in range(len(values))
+        ]
 
     def g_gate(l):
-        m.ggn[l] = padded(dot(m.gm[l], m.wo[l], 1, 1))
+        m.ggn[l] = padded(dot(gm[l][:, 0:D], m.wo[l], 1, 1))
 
     def weight_parts(q, l, parts):
         w = q.r.shape[-1]
@@ -596,7 +626,7 @@
                 q.c.at[l, t], q.x.at[l, z], q.U.at[l, d], q.V.at[l, d], (2 * t + c, h)
             )
 
-        ring = Ring(mk, 4)
+        ring = Ring(mk, 4, lambda f: every(1, 4, f))
 
         def middle():
             pair.wait()
@@ -617,7 +647,7 @@
         v = m.v[l]
         ggn = m.ggn[l]
         rv = r * v
-        gv = r * (gain * ggn) - v * (r * r * r * s2 / INNER)
+        gv = r * (gain * ggn) - v * (r * r * s2 / INNER)
         zz = m.pj[l, G:, 512:768]
         sz = jax.nn.sigmoid(zz)
         x = m.x[l]
@@ -628,7 +658,8 @@
         begin, middle, end = chain(l, m.gl, m.gn, m.bc, 0, 1, -1)
         begin()
         m.sm[l, 5:6, 0:256] = jnp.sum(ggn * rv, axis=0, keepdims=True)
-        m.gnb[l] = (rv * gain).astype(BF16)
+        if l:
+            gate_norm(l, r)
         m.ge[l, :, 512:768] = (gv * y * (sz * (1.0 + zz * (1.0 - sz)))).astype(BF16)
         gxd = jnp.zeros((T, 256), F32)
         ds = jnp.zeros((T, T), F32)
@@ -639,7 +670,7 @@
             ds = ds + fine(g_k, xdt, 1, 1) * m.seg[l, k]
         middle()
         weight_mid, weight_end = weight_parts(
-            m.we, l, [(nx[l], m.ge[l, :, 512:768]), (m.gm.at[l], m.gnb[l])]
+            m.we, l, [(nx[l], m.ge[l, :, 512:768]), (gm[l], m.gnb[l])]
         )
         bm, cm = m.bm[l], m.cm[l]
         db = fine(ds, cm, 0, 0)
@@ -685,15 +716,6 @@
         m.sm[l, 6:7, 256:384] = gskip
         m.sm[l, 6:7, 384:512] = jnp.zeros((1, 128), F32)
         m.sm[l, 7:8, :] = jnp.zeros((1, 512), F32)
-        for kc in (0, 256):
-            gpre = m.gp[l, 0:T, kc : kc + 256]
-            for k in range(4):
-                at = G - 3 + k
-                m.sm[l, k : k + 1, kc : kc + 256] = jnp.sum(
-                    gpre * m.pj[l, at : at + T, kc : kc + 256], axis=0, keepdims=True
-                )
-            m.sm[l, 4:5, kc : kc + 256] = jnp.sum(gpre, axis=0, keepdims=True)
-
         @pl.when(s == NS - 1)
         def _():
             m.gp[l, T:, :] = jnp.zeros((G, 512), F32)
@@ -717,7 +739,7 @@
                 dot(m.ge[l, :, 0:C], m.wz[l, 1, :, at], 1, 0)
                 + dot(m.ge[l, :, 512 : 512 + C], m.wz[l, 0, :, at], 1, 0)
                 + dot(m.ge[l, :, 256:512], m.wb[l, at, :], 1, 1)
-                + dot(low, wd_ref[l, :, at], 1, 0)
+                + dot(low, m.wd[l, :, at], 1, 0)
             )
             if l == 0:
                 m.ngp[l, 0:1, at] = jnp.sum(part * (m.hid[:, at] * m.q0[:, 0:1]), axis=0, keepdims=True)
@@ -727,6 +749,14 @@
         )
         ring.start()
         m.gqr[l, h] = m.gq[l, rows16(h), :]
+        for kc in (0, 256):
+            gpre = m.gp[l, 0:T, kc : kc + 256]
+            for k in range(4):
+                at = G - 3 + k
+                m.sm[l, k : k + 1, kc : kc + 256] = jnp.sum(
+                    gpre * m.pj[l, at : at + T, kc : kc + 256], axis=0, keepdims=True
+                )
+            m.sm[l, 4:5, kc : kc + 256] = jnp.sum(gpre, axis=0, keepdims=True)
         late()
         last_mid, last_end = weight_parts(m.wl, l, [(nx[l], m.ge[l, :, 0:256])])
 
@@ -769,7 +799,7 @@
             total = total_of(m.gbr.at[l], NH)
             m.sm[l, 0:5, 256:512] = total[R : R + 5]
             m.sm[l, 7:8, 0:256] = total[R + 5 : R + 6]
-            part = dot(total[0:R].astype(BF16), nx[l][:, 0:D], 1, 0).astype(BF16)
+            part = dot(total[0:R].astype(BF16), nx[l][...], 1, 0).astype(BF16)
             for t in range(NS):
                 m.gcs[l, t] = padded(part[:, C * t : C * t + C])
             self.b.start()
@@ -792,51 +822,63 @@
     loads[2].wait()
     forward(0, lambda: pl.semaphore_wait(bar, NH - 1 + NS - 1))
     loads[3].wait()
-    r0, o0 = mix_sum(0, mix_out(0))
-    u1 = m.hid[rows16(h), :] + r0 * o0
+    r0 = lax.rsqrt(scalars(0, m.v[0] * m.v[0])[0] / INNER + EPS)
+    m.r0[...] = jnp.broadcast_to(r0, (T, 128))
+    rest = gate_norm(0, r0)[:, 0:C].astype(BF16)
+    end0 = mix_out(0)
+    for j in range(3):
+        at = slice(512 * j, 512 * j + 512)
+        m.lo[:, at] = dot(rest, m.wo[0, :, at], 1, 0).astype(BF16)
+    o0 = end0()
+    m.orow[...] = o0
+    u1 = m.hid[rows16(h), :] + o0
     m.urow[...] = u1
-    m.nx1[rows16(h), 0:D] = norm_rows(u1, 1)[1]
-    m.nx1[rows16(h), D:] = scalar_lanes(r0)
+    m.nx1[rows16(h), :] = norm_rows(u1, 1)[1]
     ag = head_ring(lambda t: m.nx1.at[rows16(h)], lambda me: m.nx1.at[rows16(me)], m.agq)
     ag.start()
 
     for cp in loads[4:]:
         cp.wait()
-    m.gm[1] = m.og[...].astype(BF16)
+    m.gm1[...] = m.og[...].astype(BF16)
     g_gate(1)
     ag.wait()
 
+    low = head_ring(lambda t: m.lo.at[rows16(t)], lambda me: m.lor.at[me], m.loq)
+    low.start()
+    m.lor[h] = m.lo[rows16(h), :]
     forward(1, lambda: None)
-    cols = scalars(1)()
-    r1 = lax.rsqrt(cols[:, 0:1] / INNER + EPS)
+    v = m.v[1]
+    sq, s2 = scalars(1, v * v, m.ggn[1] * (sp[1, 5:6, 0:256] * v))
+    r1 = lax.rsqrt(sq / INNER + EPS)
     rings = []
 
     def hidden_rows():
-        rr, oo = mix_sum(1, rings[0])
-        final = m.urow[...] + rr * oo
+        final = m.urow[...] + rings[0]()
         for t in range(NH):
             m.hos[t] = padded(final[:, S * t : S * t + S], 128)
 
     back1, e1_end, l1_mid, l1_end = backward(
-        1, r1, cols[:, 1:2], lambda: rings.append(mix_out(1)), lambda: None
+        1, r1, r1 * s2, lambda: rings.append(mix_out(1)), lambda: None
     )
     l1_mid()
     hidden_rows()
+    low.wait()
+    m.orow[...] = m.orow[...] + total_of(m.lor, NH)
     g_rows = norm_back(1, m.urow[...], m.og[rows16(h), :], back1())
     m.grow[...] = g_rows
-    m.gm[0, rows16(h), :] = g_rows.astype(BF16)
-    agm = head_ring(
-        lambda t: m.gm.at[0, rows16(h)], lambda me: m.gm.at[0, rows16(me)], m.gmq
+    rounded = g_rows.astype(BF16)
+    m.gm0[rows16(h), 0:D] = rounded
+    m.gm0[rows16(h), D:] = scalar_lanes(
+        jnp.sum(rounded.astype(F32) * m.orow[...], axis=1, keepdims=True)
     )
+    agm = head_ring(lambda t: m.gm0.at[rows16(h)], lambda me: m.gm0.at[rows16(me)], m.gmq)
     agm.start()
-    ex = m.nx1[:, D:].astype(F32)
-    r0 = ex[:, 0:1] + ex[:, 1:2]
     e1_end(256)
     l1_end(0)
     agm.wait()
 
     g_gate(0)
-    cols = scalars(0)()
+    s2 = m.gm0[:, D:].astype(F32)
     hor = head_ring(lambda t: m.hos.at[t], lambda me: ho.at[rows16(me)], m.hoq)
 
     def early0():
@@ -844,7 +886,7 @@
         ho[rows16(h), :] = m.hos[h]
         small[1].first()
 
-    back0, e0_end, l0_mid, l0_end = backward(0, r0, cols[:, 1:2], early0, small[0].first)
+    back0, e0_end, l0_mid, l0_end = backward(0, m.r0[:, 0:1], s2[:, 0:1] + s2[:, 1:2], early0, small[0].first)
     small[1].second()
     small[0].second()
     l0_mid()
@@ -866,7 +908,15 @@
         f()
 
 
-def arrange(ho, gi, w, bct, smo, o_ho, o_gi, o_ng, o_zx, o_bc, o_dt, o_cx, o_cb, o_hp, o_gg, o_wo):
+def arrange(
+    ho_in, gi_in, w_in, bct_in, smo_in, o_ho, o_gi, o_ng, o_zx, o_bc, o_dt, o_cx, o_cb, o_hp, o_gg, o_wo, ho, gi, w, bct, smo, sems
+):
+    pairs = ((w_in, w), (ho_in, ho), (gi_in, gi), (bct_in, bct), (smo_in, smo))
+    copies = [pltpu.make_async_copy(a, b, sems.at[i]) for i, (a, b) in enumerate(pairs)]
+    for cp in copies:
+        cp.start()
+    for cp in copies:
+        cp.wait()
     o_ho[...] = jnp.transpose(ho[...])[0:S, :]
     o_gi[...] = jnp.transpose(gi[...])[0:S, :]
     for l in range(2):
@@ -899,7 +949,6 @@
     w_out,
     out_grad,
 ):
-    wd = jnp.pad(jnp.transpose(w_dt, (0, 2, 1)), ((0, 0), (0, R - 3), (0, 0)))
     whole = pl.BlockSpec(memory_space=pltpu.VMEM)
     there = pl.BlockSpec(memory_space=pl.ANY)
 
@@ -930,7 +979,7 @@
         jnp.transpose(conv_bc, (1, 0, 2)),
         jnp.transpose(head_params, (1, 0, 2)),
         gate_gain,
-        wd,
+        jnp.transpose(w_dt, (2, 0, 1)),
         jnp.transpose(gate_mixer_weight, (0, 2, 3, 1)),
         w_bc,
         w_out,
@@ -950,9 +999,10 @@
             out(2, C),
             out(2, C, C),
         ],
-        in_specs=[whole] * 5,
+        in_specs=[there] * 5,
         out_specs=[whole] * 11,
-        compiler_params=pltpu.CompilerParams(vmem_limit_bytes=40 * 2**20),
+        scratch_shapes=[vm(T, 128), vm(T, 128), vm(2, C, 768), half(2, NH, R, 256), vm(2, 8, 512), sem(5)],
+        compiler_params=pltpu.CompilerParams(vmem_limit_bytes=60 * 2**20),
         name="arrange",
     )(*raw)
     return (

time: 156 us -> 156 us (level)
  local copies, waits for them, and re-layouts: 6.16 us -> 0 us
  Pallas kernels: 149 us -> 155 us
    unnamed x11 -> x0, local copies, waits for them, and re-layouts: 5.51 us -> none
    pallas_call x1, Pallas kernels: 147 us -> 152 us  [on_device(): pl.pallas_call(kernel, out_shape=[out(T, 128), out(T, 128), out(2, C, 768...]
where the time goes in v3:
time: 156 us
  Pallas kernels  155 us (99%)
    pallas_call x1, Pallas kernels, on_device(): pl.pallas_call(kernel, out_shape=[out(T, 128), out(T, 128), out(2, C, 768...  152 us

profile of v3, /device:TPU:1, one launch (start us, length us, event | category | flops | bytes accessed | tf_op | source)
XLA Modules:
  0.0 155.9 jit_solution(9985568906662622156)
XLA Ops:
  0.6 152.0 %two_layers.1 = (f32[256,128]{1,0:T(8,128)}, f32[256,128]{1,0:T(8,128)}, f32[2,192,768]{2,1,0:T(8,128)}, bf16[2,16,16,256]{3,2,1,0:T(8,128)(2,1)}, f32[2,8,512]{2,1,0:T(8,128)}) custom-call(f32[256,1536]{1,0:T(8,128)} %hid_in.1, f32[256,1536]{1,0:T(8,128)} %og_in.1, f32[2,1536]{1,0:T(2,128)} %ng_ref.1, f32[5,2,192]{2,1,0:T(2,128)} %bitcast.13, ...), custom_call_target="tpu_custom_call" | custom-call | tf_op jit(solution)/shard_map/two_layers/pallas_call | solution.py:958
  152.7 3.1 %arrange.1 = (f32[96,256]{1,0:T(8,128)}, f32[96,256]{1,0:T(8,128)}, f32[2,96]{1,0:T(2,128)}, f32[2,192,2,192]{3,2,1,0:T(2,128)}, f32[2,192,256]{2,1,0:T(8,128)},...) custom-call(f32[256,128]{1,0:T(8,128)} %get-tuple-element.27.ho_in, ...), custom_call_target="tpu_custom_call" | custom-call | tf_op jit(solution)/shard_map/arrange/pallas_call | solution.py:987

commit v4 on v3

--- a/solution.py
+++ b/solution.py
@@ -9,7 +9,6 @@
 
 EPS = 1e-05
 MESH = pl.DeviceIdType.MESH
-HI = lax.Precision.HIGHEST
 F32 = jnp.float32
 BF16 = jnp.bfloat16
 
@@ -26,14 +25,8 @@
 S = D // NH
 
 
-def dot(a, b, ca, cb, precise=False):
-    return lax.dot_general(
-        a,
-        b,
-        (((ca,), (cb,)), ((), ())),
-        precision=HI if precise else None,
-        preferred_element_type=F32,
-    )
+def dot(a, b, ca, cb):
+    return lax.dot_general(a, b, (((ca,), (cb,)), ((), ())), preferred_element_type=F32)
 
 
 def halves(a):
@@ -51,6 +44,12 @@
                 term = dot(p, q, ca, cb)
                 total = term if total is None else total + term
     return total
+
+
+def sums(ones, value, ca, cb):
+    hi, lo = halves(value)
+    rest = (value - hi.astype(F32) - lo.astype(F32)).astype(BF16)
+    return dot(ones, hi, ca, cb) + dot(ones, lo, ca, cb) + dot(ones, rest, ca, cb)
 
 
 def iota(shape, dim):
@@ -167,7 +166,11 @@
     fc=chain_refs(),
     bc=chain_refs(),
     op0=vm(T, D),
-    opr0=vm(NH, R, D),
+    oph=half(T, D),
+    opr0=half(NH, R, D),
+    opl=half(T, D),
+    oplr=half(NH, R, D),
+    oplq=both(NH),
     op1=half(T, D),
     opr1=half(NH, R, D),
     opq=both(2, NH),
@@ -177,7 +180,7 @@
     r0=vm(T, 128),
     urow=vm(R, D),
     orow=vm(R, D),
-    agq=both(NH),
+    agq=dict(LS=sem(NH), LR=sem(NH), RS=sem(NH), RR=sem(NH)),
     scs=vm(2, 8, 128),
     scr=vm(2, NH, 8, 128),
     scq=both(2, NH),
@@ -185,7 +188,7 @@
     hoq=both(NH),
     gm0=half(T, X),
     gm1=half(T, D),
-    gmq=both(NH),
+    gmq=dict(LS=sem(NH), LR=sem(NH), RS=sem(NH), RR=sem(NH)),
     ggn=vm(2, T, 256),
     gnb=half(2, T, 256),
     gp=vm(2, T + G, 512),
@@ -200,9 +203,12 @@
     fas=vm(NH, R, 128),
     faq=both(NH),
     sm=vm(2, 8, 512),
-    gbs=vm(2, NH, R + G, 256),
-    gbr=vm(2, NH, R + G, 256),
+    gbs=vm(2, NH, R, 256),
+    gbr=vm(2, NH, R, 256),
     gbq=both(2, NH),
+    gss=vm(2, NH, G, 256),
+    gsr=vm(2, NH, G, 256),
+    gsq=both(2, NH),
     smr=vm(2, NS, 8, 512),
     smq=both(2, NS),
     gcs=half(2, NS, R, 256),
@@ -375,9 +381,10 @@
     lane256 = iota((T, 256), 1)
     head_lane = [jnp.logical_and(lane256 >= 64 * k, lane256 < 64 * k + 64) for k in range(3)]
     causal = iota((T, T), 0) >= iota((T, T), 1)
-    tri = jnp.where(causal, 1.0, 0.0)
+    tri = jnp.where(causal, 1.0, 0.0).astype(BF16)
     ecol = jnp.where(iota((256, 128), 0) // 64 == iota((256, 128), 1), 1.0, 0.0)
     ecol = jnp.where(iota((256, 128), 1) < 3, ecol, 0.0)
+    ecolb = ecol.astype(BF16)
 
     def only(k, a):
         return jnp.where(head_lane[k], a, jnp.zeros_like(a))
@@ -409,7 +416,7 @@
                 jnp.logical_and(c == near, gets),
             )
 
-        B = [link(d) for d in (1, 2, 3)]
+        B = [link(d) for d in (2, 1, 3)]
         first = z == 0 if step > 0 else z == 3
         more = jnp.logical_not(first)
         Cc = One(
@@ -503,7 +510,7 @@
         m.pj[l, G:, 512:768] = padded(dot(n, m.wz[l, 0], 1, 1))
         dt = jnp.where(dt_lane, jax.nn.softplus(m.pjd[l] + sp[l, 6:7, 0:128]), 0.0)
         la = -dt * jnp.exp(sp[l, 7:8, 0:128])
-        cum = dot(tri, la, 1, 0, True)
+        cum = sums(tri, la, 1, 0)
         m.dt[l] = dt
         m.cum[l] = cum
         dtb = spread(dt)
@@ -556,20 +563,75 @@
         m.gnb[l] = exact.astype(BF16)
         return exact - m.gnb[l].astype(F32)
 
+    def gather_rows(buf, cut, width, q):
+        def place(dx, dy):
+            return (hx + dx) % 4 * 4 + (hy + dy) % 4
+
+        def left(d):
+            dx, dy = d // 4, d % 4
+            source = rows16(jnp.where(dy == 0, h, place(4 - dx, 0)))
+            to = jnp.where(dy == 0, place(dx, 0), place(0, dy))
+            part = buf.at[source, pl.ds(0, cut)]
+            return rdma(part, part, q.LS.at[d], q.LR.at[d], (s, to))
+
+        def right(d):
+            dx, dy = d // 4, d % 4
+            source = rows16(jnp.where(dx == 0, h, place(0, 4 - dy)))
+            to = jnp.where(dx == 0, place(0, dy), place(dx, 0))
+            part = buf.at[source, pl.ds(cut, width - cut)]
+            return rdma(part, part, q.RS.at[d], q.RR.at[d], (s, to))
+
+        def all_sent():
+            every(1, NH, lambda d: left(d).wait_send())
+            every(1, NH, lambda d: right(d).wait_send())
+
+        finals.append(all_sent)
+        order = (2, 1, 3)
+        for k in order:
+            left(4 * k).start()
+            right(k).start()
+        for k in order:
+            left(k).start()
+            right(4 * k).start()
+
+        def end():
+            for k in (1, 3, 2):
+                left(4 * k).wait_recv()
+                for j in order:
+                    left(4 * k + j).start()
+                right(k).wait_recv()
+                for j in order:
+                    right(4 * j + k).start()
+
+            def rest(d):
+                @pl.when(d % 4 > 0)
+                def _():
+                    left(d).wait_recv()
+
+                @pl.when(d // 4 > 0)
+                def _():
+                    right(d).wait_recv()
+
+            every(1, NH, rest)
+
+        return end
+
+    def rows_sum(src, dst, q, lead=()):
+        ring = head_ring(lambda t: src.at[rows16(t)], lambda me: dst.at[me], q, lead)
+        ring.start()
+        dst[h] = src[rows16(h), :]
+
+        def end():
+            ring.wait()
+            return total_of(dst, NH)
+
+        return end
+
     def mix_out(l):
-        op, opr = ((m.op0, m.opr0), (m.op1, m.opr1))[l]
         for j in range(3):
             at = slice(512 * j, 512 * j + 512)
-            op[:, at] = dot(m.gnb[l, :, 0:C], m.wo[l, :, at], 1, 0).astype(op.dtype)
-        ring = head_ring(lambda t: op.at[rows16(t)], lambda me: opr.at[me], m.opq, (l,))
-        ring.start()
-        opr[h] = op[rows16(h), :]
-
-        def end():
-            ring.wait()
-            return total_of(opr, NH)
-
-        return end
+            m.op1[:, at] = dot(m.gnb[l, :, 0:C], m.wo[l, :, at], 1, 0).astype(BF16)
+        return rows_sum(m.op1, m.opr1, m.opq, (l,))
 
     def total_of(ref, count):
         total = ref[0].astype(F32)
@@ -577,18 +639,19 @@
             total = total + ref[t].astype(F32)
         return total
 
-    def scalars(i, *values):
-        ones = jnp.full((8, 256), 1.0, F32)
+    def scalars(i, *values, beside=lambda: None):
+        ones = jnp.full((R, 256), 1.0, BF16)
         row = iota((8, 128), 0)
         packed = jnp.zeros((8, 128), F32)
         for k, value in enumerate(values):
-            sums = dot(ones, value, 1, 1, True)
-            packed = jnp.where(row == 2 * k, sums[:, 0:128], packed)
-            packed = jnp.where(row == 2 * k + 1, sums[:, 128:256], packed)
+            over = sums(ones, value, 1, 1)[0:8]
+            packed = jnp.where(row == 2 * k, over[:, 0:128], packed)
+            packed = jnp.where(row == 2 * k + 1, over[:, 128:256], packed)
         m.scs[i] = packed
         ring = head_ring(lambda t: m.scs.at[i], lambda me: m.scr.at[i, me], m.scq, (i,))
         ring.start()
         m.scr[i, h] = m.scs[i]
+        beside()
         ring.wait()
         total = total_of(m.scr.at[i], NH)
         cols = jnp.transpose(jnp.concatenate([total, jnp.zeros((120, 128), F32)], axis=0))
@@ -618,7 +681,6 @@
             yes,
             yes,
         )
-        pair.start()
 
         def mk(d):
             t = lax.rem(z + d, 4)
@@ -639,9 +701,9 @@
             ring.wait()
             wout[l, :, col : col + w] = total_of(q.x.at[l], 4)
 
-        return middle, end
-
-    def backward(l, r, s2, early, late):
+        return pair.start, middle, end
+
+    def backward(l, r, s2, early, late, last_of_all):
         gain = sp[l, 5:6, 0:256]
         skip = spread(sp[l, 8:9, 0:128])
         v = m.v[l]
@@ -669,18 +731,16 @@
             gxd = gxd + fine(m.vw[l, k], g_k, 0, 0)
             ds = ds + fine(g_k, xdt, 1, 1) * m.seg[l, k]
         middle()
-        weight_mid, weight_end = weight_parts(
+        weight_go, weight_mid, weight_end = weight_parts(
             m.we, l, [(nx[l], m.ge[l, :, 512:768]), (gm[l], m.gnb[l])]
         )
         bm, cm = m.bm[l], m.cm[l]
         db = fine(ds, cm, 0, 0)
         dc = fine(ds, bm, 1, 0) + fine(gyc, m.hin[l], 1, 0)
-        dcum = dot(gy * m.yn[l], ecol, 1, 0, True)
-        col_in = dot(xdt * gxd, ecol, 1, 0, True)
-        gskip = jnp.sum(dot(gy * x, ecol, 1, 0, True), axis=0, keepdims=True)
+        gskip = jnp.sum(gy * x, axis=0, keepdims=True)
         early()
         end()
-        weight_mid()
+        weight_go()
         gnx = m.gn[l]
         db = db + fine(m.xtail[l], gnx, 1, 0)
         rt = m.etb[l] * fine(bm, gnx, 1, 1)
@@ -698,22 +758,27 @@
         )
         halo.start()
         dt = m.dt[l]
-        tail = dot(x * rt, ecol, 1, 0, True)
-        gdt = dot(x * gxs, ecol, 1, 0, True)
-        tail = dt * tail
+        gdt = fine(x * gxs, ecolb, 1, 0)
         cum = m.cum[l]
         inner = jnp.sum(gnx * m.hin[l], axis=1, keepdims=True)
         inner = jnp.sum(inner * ecol, axis=0, keepdims=True)
-        last = jnp.sum(tail, axis=0, keepdims=True) + jnp.exp(cum[T - 1 : T, :]) * inner
-        dcum = dcum - col_in - tail + jnp.where(iota((T, 128), 0) == T - 1, last, 0.0)
-        gla = dot(tri, dcum, 0, 0, True)
+        tail = jnp.sum(xdt * rt, axis=0, keepdims=True)
+        both = fine(jnp.concatenate([tail, gskip, jnp.zeros((6, 256), F32)], axis=0), ecolb, 1, 0)
+        last = both[0:1] + jnp.exp(cum[T - 1 : T, :]) * inner
+        pairs = gy * m.yn[l] - xdt * gxs
+        hi, lo = halves(pairs)
+        rest = (pairs - hi.astype(F32) - lo.astype(F32)).astype(BF16)
+        dcum = fine(pairs, ecolb, 1, 0) + dot(rest, ecolb, 1, 0)
+        dcum = dcum + jnp.where(iota((T, 128), 0) == T - 1, last, 0.0)
+        gla = sums(tri, dcum, 0, 0)
         rate = jnp.exp(sp[l, 7:8, 0:128])
         gd = gdt - gla * rate
         gdtr = jnp.where(dt_lane, gd * jax.nn.sigmoid(m.pjd[l] + sp[l, 6:7, 0:128]), 0.0)
+        weight_mid()
         m.sm[l, 5:6, 256:512] = jnp.zeros((1, 256), F32)
         m.sm[l, 6:7, 0:128] = jnp.sum(gdtr, axis=0, keepdims=True)
         m.sm[l, 6:7, 128:256] = jnp.sum(-gla * dt * rate, axis=0, keepdims=True)
-        m.sm[l, 6:7, 256:384] = gskip
+        m.sm[l, 6:7, 256:384] = both[1:2]
         m.sm[l, 6:7, 384:512] = jnp.zeros((1, 128), F32)
         m.sm[l, 7:8, :] = jnp.zeros((1, 512), F32)
         @pl.when(s == NS - 1)
@@ -730,8 +795,9 @@
             else:
                 gt = jnp.transpose(gj)
                 for t in range(NH):
-                    m.gbs[l, t, 0:R, :] = gt[R * t : R * t + R, :]
+                    m.gbs[l, t] = gt[R * t : R * t + R, :]
             m.ge[l, :, kc : kc + 256] = gj.astype(BF16)
+        late()
         low = gdtr[:, 0:R].astype(BF16)
         for j in range(3):
             at = slice(512 * j, 512 * j + 512)
@@ -757,8 +823,9 @@
                     gpre * m.pj[l, at : at + T, kc : kc + 256], axis=0, keepdims=True
                 )
             m.sm[l, 4:5, kc : kc + 256] = jnp.sum(gpre, axis=0, keepdims=True)
-        late()
-        last_mid, last_end = weight_parts(m.wl, l, [(nx[l], m.ge[l, :, 0:256])])
+        last_of_all()
+        last_go, last_mid, last_end = weight_parts(m.wl, l, [(nx[l], m.ge[l, :, 0:256])])
+        last_go()
 
         def finish():
             ring.wait()
@@ -779,32 +846,45 @@
             self.a = head_ring(
                 lambda t: m.gbs.at[l, t], lambda me: m.gbr.at[l, me], m.gbq, (l,)
             )
+            self.e = head_ring(
+                lambda t: m.gss.at[l, t], lambda me: m.gsr.at[l, me], m.gsq, (l,)
+            )
             self.b = seq_ring(lambda t: m.gcs.at[l, t], lambda me: m.gcr.at[l, me], m.gcq, (l,))
             self.c = seq_ring(lambda t: m.sm.at[l], lambda me: m.smr.at[l, me], m.smq, (l,))
             self.d = head_ring(lambda t: m.gds.at[l], lambda me: bct.at[l, me], m.gdq, (l,))
 
         def first(self):
             l = self.l
-            for t in range(NH):
-                m.gbs[l, t, R : R + 5, :] = m.sm[l, 0:5, 256:512]
-                m.gbs[l, t, R + 5 : R + 6, 0:S] = m.ngp[l, 0:1, S * t : S * t + S]
-                m.gbs[l, t, R + 5 : R + 6, S:] = jnp.zeros((1, 256 - S), F32)
-                m.gbs[l, t, R + 6 :, :] = jnp.zeros((2, 256), F32)
             self.a.start()
             m.gbr[l, h] = m.gbs[l, h]
+
+        def first_small(self):
+            l = self.l
+            for t in range(NH):
+                m.gss[l, t, 0:5, :] = m.sm[l, 0:5, 256:512]
+                m.gss[l, t, 5:6, 0:S] = m.ngp[l, 0:1, S * t : S * t + S]
+                m.gss[l, t, 5:6, S:] = jnp.zeros((1, 256 - S), F32)
+                m.gss[l, t, 6:, :] = jnp.zeros((2, 256), F32)
+            self.e.start()
+            m.gsr[l, h] = m.gss[l, h]
 
         def second(self):
             l = self.l
             self.a.wait()
             total = total_of(m.gbr.at[l], NH)
-            m.sm[l, 0:5, 256:512] = total[R : R + 5]
-            m.sm[l, 7:8, 0:256] = total[R + 5 : R + 6]
-            part = dot(total[0:R].astype(BF16), nx[l][...], 1, 0).astype(BF16)
+            part = dot(total.astype(BF16), nx[l][...], 1, 0).astype(BF16)
             for t in range(NS):
                 m.gcs[l, t] = padded(part[:, C * t : C * t + C])
             self.b.start()
+            m.gcr[l, s] = m.gcs[l, s]
+
+        def second_small(self):
+            l = self.l
+            self.e.wait()
+            total = total_of(m.gsr.at[l], NH)
+            m.sm[l, 0:5, 256:512] = total[0:5]
+            m.sm[l, 7:8, 0:256] = total[5:6]
             self.c.start()
-            m.gcr[l, s] = m.gcs[l, s]
             m.smr[l, s] = m.sm[l]
 
         def third(self):
@@ -813,8 +893,10 @@
             m.gds[l] = total_of(m.gcr.at[l], NS).astype(BF16)
             self.d.start()
             bct[l, h] = m.gds[l]
+
+        def third_small(self):
             self.c.wait()
-            smo[l] = total_of(m.smr.at[l], NS)
+            smo[self.l] = total_of(m.smr.at[self.l], NS)
 
     small = [Small(0), Small(1)]
 
@@ -822,26 +904,38 @@
     loads[2].wait()
     forward(0, lambda: pl.semaphore_wait(bar, NH - 1 + NS - 1))
     loads[3].wait()
-    r0 = lax.rsqrt(scalars(0, m.v[0] * m.v[0])[0] / INNER + EPS)
+    ends = []
+
+    def high_parts():
+        vg = (m.v[0] * sp[0, 5:6, 0:256])[:, 0:C]
+        for j in range(3):
+            at = slice(512 * j, 512 * j + 512)
+            m.op0[:, at] = fine(vg, m.wo[0, :, at], 1, 0)
+            m.oph[:, at] = m.op0[:, at].astype(BF16)
+        ends.append(rows_sum(m.oph, m.opr0, m.opq, (0,)))
+
+    sq = scalars(0, m.v[0] * m.v[0], beside=high_parts)[0]
+    r0 = lax.rsqrt(sq / INNER + EPS)
     m.r0[...] = jnp.broadcast_to(r0, (T, 128))
     rest = gate_norm(0, r0)[:, 0:C].astype(BF16)
-    end0 = mix_out(0)
     for j in range(3):
         at = slice(512 * j, 512 * j + 512)
-        m.lo[:, at] = dot(rest, m.wo[0, :, at], 1, 0).astype(BF16)
-    o0 = end0()
+        left = dot(rest, m.wo[0, :, at], 1, 0)
+        m.lo[:, at] = left.astype(BF16)
+        m.opl[:, at] = (r0 * (m.op0[:, at] - m.oph[:, at].astype(F32)) - left).astype(BF16)
+    ends.append(rows_sum(m.opl, m.oplr, m.oplq))
+    o0 = m.r0[rows16(h), 0:1] * ends[0]() + ends[1]()
     m.orow[...] = o0
     u1 = m.hid[rows16(h), :] + o0
     m.urow[...] = u1
     m.nx1[rows16(h), :] = norm_rows(u1, 1)[1]
-    ag = head_ring(lambda t: m.nx1.at[rows16(h)], lambda me: m.nx1.at[rows16(me)], m.agq)
-    ag.start()
+    ag_end = gather_rows(m.nx1, D // 2, D, m.agq)
 
     for cp in loads[4:]:
         cp.wait()
     m.gm1[...] = m.og[...].astype(BF16)
     g_gate(1)
-    ag.wait()
+    ag_end()
 
     low = head_ring(lambda t: m.lo.at[rows16(t)], lambda me: m.lor.at[me], m.loq)
     low.start()
@@ -858,7 +952,7 @@
             m.hos[t] = padded(final[:, S * t : S * t + S], 128)
 
     back1, e1_end, l1_mid, l1_end = backward(
-        1, r1, r1 * s2, lambda: rings.append(mix_out(1)), lambda: None
+        1, r1, r1 * s2, lambda: rings.append(mix_out(1)), lambda: None, lambda: None
     )
     l1_mid()
     hidden_rows()
@@ -871,11 +965,10 @@
     m.gm0[rows16(h), D:] = scalar_lanes(
         jnp.sum(rounded.astype(F32) * m.orow[...], axis=1, keepdims=True)
     )
-    agm = head_ring(lambda t: m.gm0.at[rows16(h)], lambda me: m.gm0.at[rows16(me)], m.gmq)
-    agm.start()
+    agm_end = gather_rows(m.gm0, D // 2, X, m.gmq)
     e1_end(256)
     l1_end(0)
-    agm.wait()
+    agm_end()
 
     g_gate(0)
     s2 = m.gm0[:, D:].astype(F32)
@@ -885,19 +978,24 @@
         hor.start()
         ho[rows16(h), :] = m.hos[h]
         small[1].first()
-
-    back0, e0_end, l0_mid, l0_end = backward(0, m.r0[:, 0:1], s2[:, 0:1] + s2[:, 1:2], early0, small[0].first)
+        small[1].first_small()
+
+    back0, e0_end, l0_mid, l0_end = backward(0, m.r0[:, 0:1], s2[:, 0:1] + s2[:, 1:2], early0, small[0].first, small[0].first_small)
     small[1].second()
+    small[1].second_small()
     small[0].second()
     l0_mid()
+    small[0].second_small()
     small[1].third()
+    small[0].third()
     g_rows = norm_back(0, m.hid[rows16(h), :], m.grow[...], back0())
     for t in range(NH):
         m.fas[t] = padded(g_rows[:, S * t : S * t + S], 128)
     far = head_ring(lambda t: m.fas.at[t], lambda me: gi.at[rows16(me)], m.faq)
     far.start()
     gi[rows16(h), :] = m.fas[h]
-    small[0].third()
+    small[1].third_small()
+    small[0].third_small()
     e0_end(256)
     l0_end(0)
     hor.wait()

time: 156 us -> 142 us (0.910)
  Pallas kernels: 155 us -> 141 us
    pallas_call x1, Pallas kernels: 152 us -> 138 us  [on_device(): pl.pallas_call(kernel, out_shape=[out(T, 128), out(T, 128), out(2, C, 768...]
where the time goes in v4:
time: 142 us
  Pallas kernels  141 us (99%)
    pallas_call x1, Pallas kernels, on_device(): pl.pallas_call(kernel, out_shape=[out(T, 128), out(T, 128), out(2, C, 768...  138 us
    pallas_call x1, Pallas kernels, on_device(): pl.pallas_call(arrange, out_shape=[out(S, T), out(S, T), out(2, S), out(2...  3.07 us

profile of v4, /device:TPU:1, one launch (start us, length us, event | category | flops | bytes accessed | tf_op | source)
XLA Modules:
  0.0 141.6 jit_solution(13976629229072900512)
XLA Ops:
  0.6 137.7 %two_layers.1 = (f32[256,128]{1,0:T(8,128)}, f32[256,128]{1,0:T(8,128)}, f32[2,192,768]{2,1,0:T(8,128)}, bf16[2,16,16,256]{3,2,1,0:T(8,128)(2,1)}, f32[2,8,512]{2,1,0:T(8,128)}) custom-call(f32[256,1536]{1,0:T(8,128)} %hid_in.1, f32[256,1536]{1,0:T(8,128)} %og_in.1, f32[2,1536]{1,0:T(2,128)} %ng_ref.1, f32[5,2,192]{2,1,0:T(2,128)} %bitcast.13, ...), custom_call_target="tpu_custom_call" | custom-call | tf_op jit(solution)/shard_map/two_layers/pallas_call | solution.py:1056
  138.3 3.1 %arrange.1 = (f32[96,256]{1,0:T(8,128)}, f32[96,256]{1,0:T(8,128)}, f32[2,96]{1,0:T(2,128)}, f32[2,192,2,192]{3,2,1,0:T(2,128)}, f32[2,192,256]{2,1,0:T(8,128)},...) custom-call(f32[256,128]{1,0:T(8,128)} %get-tuple-element.27.ho_in, ...), custom_call_target="tpu_custom_call" | custom-call | tf_op jit(solution)/shard_map/arrange/pallas_call | solution.py:1085

commit v5 on v4

--- a/solution.py
+++ b/solution.py
@@ -218,7 +218,17 @@
     gdq=both(2, NH),
     we=weight_refs(512),
     wl=weight_refs(256),
-    loc=sem(8),
+    ngv=vm(2, D),
+    cxv=vm(5, 2, C),
+    cbv=vm(5, 2, 256),
+    hpv=vm(3, 2, 3),
+    ggv=vm(2, C),
+    hov=vm(T, 128),
+    giv=vm(T, 128),
+    wv=vm(2, C, 768),
+    bctv=half(2, NH, R, 256),
+    smov=vm(2, 8, 512),
+    loc=sem(18),
 )
 LEAVES, TREE = jax.tree.flatten(SCRATCH)
 
@@ -226,20 +236,20 @@
 def kernel(
     hid_in,
     og_in,
-    ng_ref,
-    cx_ref,
-    cb_ref,
-    hp_ref,
-    gg_ref,
+    ng_in,
+    cx_in,
+    cb_in,
+    hp_in,
+    gg_in,
     wd_ref,
     wz_in,
     wb_in,
     wo_in,
-    ho,
-    gi,
-    wout,
-    bct,
-    smo,
+    ho_out,
+    gi_out,
+    w_out,
+    bct_out,
+    smo_out,
     *scratch,
 ):
     m = SimpleNamespace(
@@ -280,14 +290,8 @@
             every(1, self.size, lambda d: self.mk(d).wait_recv())
 
     def far_first(f):
-        def step(i):
-            d = (6 - i // 4) % 4 * 4 + (6 - i % 4) % 4
-
-            @pl.when(d > 0)
-            def _():
-                f(d)
-
-        every(0, NH, step)
+        for d in (10, 6, 9, 14, 11, 5, 15, 7, 13, 8, 2, 4, 1, 12, 3):
+            f(d)
 
     def head_ring(src, dst, q, lead=()):
         def mk(d):
@@ -327,6 +331,17 @@
     def rows16(t):
         return pl.ds(pl.multiple_of(t * R, R), R)
 
+    ng_ref, cx_ref, cb_ref, hp_ref, gg_ref = m.ngv, m.cxv, m.cbv, m.hpv, m.ggv
+    ho, gi, wout, bct, smo = m.hov, m.giv, m.wv, m.bctv, m.smov
+
+    few = [
+        pltpu.make_async_copy(a, b, m.loc.at[8 + i])
+        for i, (a, b) in enumerate(
+            zip((cx_in, cb_in, hp_in, gg_in, ng_in), (cx_ref, cb_ref, hp_ref, gg_ref, ng_ref))
+        )
+    ]
+    for cp in few:
+        cp.start()
     loads = [
         pltpu.make_async_copy(hid_in, m.hid, m.loc.at[0]),
         pltpu.make_async_copy(wz_in.at[0], m.wz.at[0], m.loc.at[1]),
@@ -349,6 +364,8 @@
     every(1, NH, lambda d: greet((s, lax.rem(h + d, NH))))
 
     m.sp[...] = jnp.zeros((2, 16, 512), F32)
+    for cp in few:
+        cp.wait()
     for l in range(2):
         for k in range(5):
             m.sp[l, k : k + 1, 0:C] = cx_ref[k, l : l + 1, :]
@@ -899,6 +916,12 @@
             smo[self.l] = total_of(m.smr.at[self.l], NS)
 
     small = [Small(0), Small(1)]
+    outs = [
+        pltpu.make_async_copy(a, b, m.loc.at[13 + i])
+        for i, (a, b) in enumerate(
+            zip((ho, gi, wout, bct, smo), (ho_out, gi_out, w_out, bct_out, smo_out))
+        )
+    ]
 
     loads[1].wait()
     loads[2].wait()
@@ -988,41 +1011,61 @@
     small[0].second_small()
     small[1].third()
     small[0].third()
+    hor.wait()
+    outs[0].start()
     g_rows = norm_back(0, m.hid[rows16(h), :], m.grow[...], back0())
     for t in range(NH):
         m.fas[t] = padded(g_rows[:, S * t : S * t + S], 128)
     far = head_ring(lambda t: m.fas.at[t], lambda me: gi.at[rows16(me)], m.faq)
     far.start()
     gi[rows16(h), :] = m.fas[h]
+    e0_end(256)
+    l0_end(0)
+    outs[2].start()
     small[1].third_small()
     small[0].third_small()
-    e0_end(256)
-    l0_end(0)
-    hor.wait()
+    outs[4].start()
     small[1].d.wait()
     small[0].d.wait()
+    outs[3].start()
     far.wait()
+    outs[1].start()
+    for cp in outs:
+        cp.wait()
     for f in finals:
         f()
 
 
-def arrange(
-    ho_in, gi_in, w_in, bct_in, smo_in, o_ho, o_gi, o_ng, o_zx, o_bc, o_dt, o_cx, o_cb, o_hp, o_gg, o_wo, ho, gi, w, bct, smo, sems
-):
-    pairs = ((w_in, w), (ho_in, ho), (gi_in, gi), (bct_in, bct), (smo_in, smo))
-    copies = [pltpu.make_async_copy(a, b, sems.at[i]) for i, (a, b) in enumerate(pairs)]
-    for cp in copies:
-        cp.start()
-    for cp in copies:
-        cp.wait()
+def arrange(*refs):
+    ins, outs, kept, forms, sems = refs[0:5], refs[5:16], refs[16:21], refs[21:32], refs[32]
+    ho, gi, w, bct, smo = kept
+    o_ho, o_gi, o_ng, o_zx, o_bc, o_dt, o_cx, o_cb, o_hp, o_gg, o_wo = forms
+    copies = [pltpu.make_async_copy(a, b, sems.at[i]) for i, (a, b) in enumerate(zip(ins, kept))]
+    back = [pltpu.make_async_copy(a, b, sems.at[5 + i]) for i, (a, b) in enumerate(zip(forms, outs))]
+    for i in (2, 3, 0, 1, 4):
+        copies[i].start()
+    copies[2].wait()
+    for l in range(2):
+        o_zx[l, :, 0, :] = w[l, :, 256 : 256 + C]
+        o_zx[l, :, 1, :] = w[l, :, 0:C]
+    back[3].start()
+    for l in range(2):
+        o_wo[l] = jnp.transpose(w[l, :, 512:768])[0:C, :]
+    back[10].start()
+    copies[3].wait()
+    for l in range(2):
+        rows = jnp.concatenate([bct[l, t].astype(F32) for t in range(NH)], axis=0)
+        o_bc[l] = jnp.transpose(rows)[0:C, :]
+    back[4].start()
+    copies[0].wait()
     o_ho[...] = jnp.transpose(ho[...])[0:S, :]
+    back[0].start()
+    copies[1].wait()
     o_gi[...] = jnp.transpose(gi[...])[0:S, :]
+    back[1].start()
+    copies[4].wait()
     for l in range(2):
         o_ng[l : l + 1, :] = smo[l, 7:8, 0:S]
-        o_zx[l, :, 0, :] = w[l, :, 256 : 256 + C]
-        o_zx[l, :, 1, :] = w[l, :, 0:C]
-        rows = jnp.concatenate([bct[l, t].astype(F32) for t in range(NH)], axis=0)
-        o_bc[l] = jnp.transpose(rows)[0:C, :]
         dts = jnp.transpose(w[l, :, 128:256])
         for k in range(3):
             o_dt[k, l : l + 1, :] = dts[64 + k : 65 + k, :]
@@ -1031,7 +1074,10 @@
             o_cx[k, l : l + 1, :] = smo[l, k : k + 1, 0:C]
             o_cb[k, l : l + 1, :] = smo[l, k : k + 1, 256:512]
         o_gg[l : l + 1, :] = smo[l, 5:6, 0:C]
-        o_wo[l] = jnp.transpose(w[l, :, 512:768])[0:C, :]
+    for i in (2, 5, 6, 7, 8, 9):
+        back[i].start()
+    for cp in back:
+        cp.wait()
 
 
 def on_device(
@@ -1062,8 +1108,8 @@
             out(2, NH, R, 256, dtype=BF16),
             out(2, 8, 512),
         ],
-        in_specs=[there] * 2 + [whole] * 6 + [there] * 3,
-        out_specs=[whole] * 5,
+        in_specs=[there] * 7 + [whole] + [there] * 3,
+        out_specs=[there] * 5,
         scratch_shapes=LEAVES,
         compiler_params=pltpu.CompilerParams(
             collective_id=0, has_side_effects=True, vmem_limit_bytes=60 * 2**20
@@ -1082,24 +1128,33 @@
         w_bc,
         w_out,
     )
+    shapes = [
+        (S, T),
+        (S, T),
+        (2, S),
+        (2, C, 2, C),
+        (2, C, 256),
+        (3, 2, C),
+        (5, 2, C),
+        (5, 2, 256),
+        (3, 2, 3),
+        (2, C),
+        (2, C, C),
+    ]
     ho, gi, ng, zx, bc, dt, cx, cb, hp, gg, wo = pl.pallas_call(
         arrange,
-        out_shape=[
-            out(S, T),
-            out(S, T),
-            out(2, S),
-            out(2, C, 2, C),
-            out(2, C, 256),
-            out(3, 2, C),
-            out(5, 2, C),
-            out(5, 2, 256),
-            out(3, 2, 3),
-            out(2, C),
-            out(2, C, C),
+        out_shape=[out(*shape) for shape in shapes],
+        in_specs=[there] * 5,
+        out_specs=[there] * 11,
+        scratch_shapes=[
+            vm(T, 128),
+            vm(T, 128),
+            vm(2, C, 768),
+            half(2, NH, R, 256),
+            vm(2, 8, 512),
+            *[vm(*shape) for shape in shapes],
+            sem(16),
         ],
-        in_specs=[there] * 5,
-        out_specs=[whole] * 11,
-        scratch_shapes=[vm(T, 128), vm(T, 128), vm(2, C, 768), half(2, NH, R, 256), vm(2, 8, 512), sem(5)],
         compiler_params=pltpu.CompilerParams(vmem_limit_bytes=60 * 2**20),
         name="arrange",
     )(*raw)

time: 142 us -> 140 us (0.986); the launches traced: 142 us -> 138 us
  Pallas kernels: 141 us -> 137 us
    pallas_call x1, Pallas kernels: 138 us -> 134 us  [on_device(): pl.pallas_call(kernel, out_shape=[out(T, 128), out(T, 128), out(2, C, 768...]
where the time goes in v5:
time: 140 us; the launch traced here: 138 us
  Pallas kernels  137 us (98%)
    pallas_call x1, Pallas kernels, on_device(): pl.pallas_call(kernel, out_shape=[out(T, 128), out(T, 128), out(2, C, 768...  134 us
    pallas_call x1, Pallas kernels, on_device(): pl.pallas_call(arrange, out_shape=[out(*shape) for shape in shapes], in_s...  3.01 us

profile of v5, /device:TPU:1, one launch (start us, length us, event | category | flops | bytes accessed | tf_op | source)
XLA Modules:
  0.0 137.8 jit_solution(16280506264099569507)
XLA Ops:
  0.6 133.9 %two_layers.1 = (f32[256,128]{1,0:T(8,128)}, f32[256,128]{1,0:T(8,128)}, f32[2,192,768]{2,1,0:T(8,128)}, bf16[2,16,16,256]{3,2,1,0:T(8,128)(2,1)}, f32[2,8,512]{2,1,0:T(8,128)}) custom-call(f32[256,1536]{1,0:T(8,128)} %hid_in.1, f32[256,1536]{1,0:T(8,128)} %og_in.1, f32[2,1536]{1,0:T(2,128)} %ng_in.1, f32[5,2,192]{2,1,0:T(2,128)} %bitcast.13, ...), custom_call_target="tpu_custom_call" | custom-call | tf_op jit(solution)/shard_map/two_layers/pallas_call | solution.py:1102
  134.6 3.0 %arrange.1 = (f32[96,256]{1,0:T(8,128)}, f32[96,256]{1,0:T(8,128)}, f32[2,96]{1,0:T(2,128)}, f32[2,192,2,192]{3,2,1,0:T(2,128)}, f32[2,192,256]{2,1,0:T(8,128)},...) custom-call(f32[256,128]{1,0:T(8,128)} %get-tuple-element.27.refs_0_, ...), custom_call_target="tpu_custom_call" | custom-call | tf_op jit(solution)/shard_map/arrange/pallas_call | solution.py:1144

commit v6 on v5

--- a/solution.py
+++ b/solution.py
@@ -142,6 +142,7 @@
     pj=vm(2, G + T, 768),
     pre=vm(2, T, 512),
     pjd=vm(2, T, 128),
+    dz=vm(2, T, 256),
     jhS=sem(2),
     jhR=sem(2),
     x=vm(2, T, 256),
@@ -720,6 +721,14 @@
 
         return pair.start, middle, end
 
+    def slopes(l):
+        zz = m.pj[l, G:, 512:768]
+        sz = jax.nn.sigmoid(zz)
+        m.pj[l, G:, 512:768] = zz * sz
+        m.dz[l] = sz * (1.0 + zz * (1.0 - sz))
+        for kc in (0, 256):
+            m.pre[l, :, kc : kc + 256] = silu_slope(m.pre[l, :, kc : kc + 256])
+
     def backward(l, r, s2, early, late, last_of_all):
         gain = sp[l, 5:6, 0:256]
         skip = spread(sp[l, 8:9, 0:128])
@@ -727,11 +736,9 @@
         ggn = m.ggn[l]
         rv = r * v
         gv = r * (gain * ggn) - v * (r * r * s2 / INNER)
-        zz = m.pj[l, G:, 512:768]
-        sz = jax.nn.sigmoid(zz)
         x = m.x[l]
         y = m.yn[l] + skip * x
-        gy = gv * (zz * sz)
+        gy = gv * m.pj[l, G:, 512:768]
         gyc = m.ecb[l] * gy
         m.gl[l] = fine(gyc, m.cm[l], 0, 0)
         begin, middle, end = chain(l, m.gl, m.gn, m.bc, 0, 1, -1)
@@ -739,7 +746,7 @@
         m.sm[l, 5:6, 0:256] = jnp.sum(ggn * rv, axis=0, keepdims=True)
         if l:
             gate_norm(l, r)
-        m.ge[l, :, 512:768] = (gv * y * (sz * (1.0 + zz * (1.0 - sz)))).astype(BF16)
+        m.ge[l, :, 512:768] = (gv * y * m.dz[l]).astype(BF16)
         gxd = jnp.zeros((T, 256), F32)
         ds = jnp.zeros((T, T), F32)
         xdt = m.xdt[l]
@@ -764,7 +771,7 @@
         gxs = gxd + rt
         gx = m.dtb[l] * gxs + skip * gy
         for kc, gpost in ((0, gx), (256, jnp.concatenate([db, dc], axis=1))):
-            gpre = gpost * silu_slope(m.pre[l, :, kc : kc + 256])
+            gpre = gpost * m.pre[l, :, kc : kc + 256]
             m.gp[l, 0:T, kc : kc + 256] = gpre
         halo = One(
             lambda: rdma(
@@ -958,6 +965,7 @@
         cp.wait()
     m.gm1[...] = m.og[...].astype(BF16)
     g_gate(1)
+    slopes(0)
     ag_end()
 
     low = head_ring(lambda t: m.lo.at[rows16(t)], lambda me: m.lor.at[me], m.loq)
@@ -965,7 +973,7 @@
     m.lor[h] = m.lo[rows16(h), :]
     forward(1, lambda: None)
     v = m.v[1]
-    sq, s2 = scalars(1, v * v, m.ggn[1] * (sp[1, 5:6, 0:256] * v))
+    sq, s2 = scalars(1, v * v, m.ggn[1] * (sp[1, 5:6, 0:256] * v), beside=lambda: slopes(1))
     r1 = lax.rsqrt(sq / INNER + EPS)
     rings = []
 

time: 140 us -> 140 us (level)
  no operation moved by 1% of the time
where the time goes in v6:
time: 140 us; the launch traced here: 138 us
  Pallas kernels  137 us (98%)
    pallas_call x1, Pallas kernels, on_device(): pl.pallas_call(kernel, out_shape=[out(T, 128), out(T, 128), out(2, C, 768...  134 us
    pallas_call x1, Pallas kernels, on_device(): pl.pallas_call(arrange, out_shape=[out(*shape) for shape in shapes], in_s...  3.01 us

profile of v6, /device:TPU:1, one launch (start us, length us, event | category | flops | bytes accessed | tf_op | source)
XLA Modules:
  0.0 138.1 jit_solution(15660628941364142268)
XLA Ops:
  0.6 134.3 %two_layers.1 = (f32[256,128]{1,0:T(8,128)}, f32[256,128]{1,0:T(8,128)}, f32[2,192,768]{2,1,0:T(8,128)}, bf16[2,16,16,256]{3,2,1,0:T(8,128)(2,1)}, f32[2,8,512]{2,1,0:T(8,128)}) custom-call(f32[256,1536]{1,0:T(8,128)} %hid_in.1, f32[256,1536]{1,0:T(8,128)} %og_in.1, f32[2,1536]{1,0:T(2,128)} %ng_in.1, f32[5,2,192]{2,1,0:T(2,128)} %bitcast.13, ...), custom_call_target="tpu_custom_call" | custom-call | tf_op jit(solution)/shard_map/two_layers/pallas_call | solution.py:1110
  134.9 3.0 %arrange.1 = (f32[96,256]{1,0:T(8,128)}, f32[96,256]{1,0:T(8,128)}, f32[2,96]{1,0:T(2,128)}, f32[2,192,2,192]{3,2,1,0:T(2,128)}, f32[2,192,256]{2,1,0:T(8,128)},...) custom-call(f32[256,128]{1,0:T(8,128)} %get-tuple-element.27.refs_0_, ...), custom_call_target="tpu_custom_call" | custom-call | tf_op jit(solution)/shard_map/arrange/pallas_call | solution.py:1152
